TPU v7x, 32 devices: a whole 2x2x4 slice. The times are simulated.
32 devices in a mesh: ctx: 16 (over z, y, core), fsdp: 2 (over x).
Axes of the slice: x: 2, y: 2, z: 4, core: 2. Of those that a mesh axis runs over, the one named last changes fastest.
Arguments:
- layer_input: bfloat16 [8, 2048, 960], P('fsdp', 'ctx'), may hold values from -6 to 6
- out_grad: bfloat16 [8, 2048, 960], P('fsdp', 'ctx'), may hold values from -6 to 6
- attn_gain: bfloat16 [960], P('fsdp'), may hold values from 0.5 to 1.5
- w_query: bfloat16 [960, 960], P('fsdp'), may hold values from -0.1875 to 0.1875
- w_key: bfloat16 [960, 320], P('fsdp'), may hold values from -0.1875 to 0.1875
- w_value: bfloat16 [960, 320], P('fsdp'), may hold values from -0.1875 to 0.1875
- w_output: bfloat16 [960, 960], P('fsdp'), may hold values from -6 to 6
- mlp_gain: bfloat16 [960], P('fsdp'), may hold values from 0.5 to 1.5
- w_gate: bfloat16 [960, 2560], P('fsdp'), may hold values from -0.1875 to 0.1875
- w_up: bfloat16 [960, 2560], P('fsdp'), may hold values from -0.1875 to 0.1875
- w_down: bfloat16 [2560, 960], P('fsdp'), may hold values from -0.125 to 0.125
Outputs:
- layer_output: bfloat16 [8, 2048, 960], P('fsdp', 'ctx')
- input_grad: bfloat16 [8, 2048, 960], P('fsdp', 'ctx')
- attn_gain_grad: float32 [960], P('fsdp')
- w_query_grad: float32 [960, 960], P('fsdp')
- w_key_grad: float32 [960, 320], P('fsdp')
- w_value_grad: float32 [960, 320], P('fsdp')
- w_output_grad: float32 [960, 960], P('fsdp')
- mlp_gain_grad: float32 [960], P('fsdp')
- w_gate_grad: float32 [960, 2560], P('fsdp')
- w_up_grad: float32 [960, 2560], P('fsdp')
- w_down_grad: float32 [2560, 960], P('fsdp')
All inputs are finite; a program needn't handle non-finite values.
Results may differ from a plain program's by a relative error of at most 0.034.
Values may be sent and summed in bfloat16 or wider, within the bound.
A program may use at most 256 MiB of HBM per device.

v0:
```python
import math

import jax
import jax.numpy as jnp
from jax import lax
from jax.sharding import PartitionSpec as P

QH = 15
KVH = 5
HD = 64


EPS = 1e-05
THETA = 100000.0
FAR = -1e30


def place_rows(start_row, row_count, shard_rows, ctx_size):
    stored = start_row + jnp.arange(row_count, dtype=jnp.int32)
    half_rows = shard_rows // 2
    holder = stored // shard_rows
    within = stored % shard_rows
    mirror = (2 * ctx_size - 1 - holder) * half_rows + within - half_rows
    return jnp.where(within < half_rows, holder * half_rows + within, mirror)


def rotate(values_in, position, heads, sign):
    full_shape = values_in.shape
    by_head = values_in.reshape(full_shape[:-1] + (heads, HD))
    frequency = THETA ** (-jnp.arange(0, HD, 2, dtype=jnp.float32) / HD)
    angles = position.astype(jnp.float32)[:, None] * frequency[None, :]
    cosine = jnp.concatenate([jnp.cos(angles), jnp.cos(angles)], -1)[:, None, :]
    sine_part = sign * jnp.concatenate([jnp.sin(angles), jnp.sin(angles)], -1)[:, None, :]
    first_half = by_head[..., : HD // 2]
    second_half = by_head[..., HD // 2 :]
    turned = jnp.concatenate([-second_half, first_half], -1)
    return (by_head * cosine + turned * sine_part).reshape(full_shape)


def to_heads(flat):
    seq_count, row_count = (flat.shape[0], flat.shape[1])
    return flat.reshape(seq_count, row_count, KVH, QH // KVH, HD).transpose(0, 2, 3, 1, 4)


def from_heads(stacked):
    seq_count, row_count = (stacked.shape[0], stacked.shape[3])
    return stacked.transpose(0, 3, 1, 2, 4).reshape(seq_count, row_count, QH * HD)


def split_kv(kv_piece):
    seq_count, row_count = (kv_piece.shape[0], kv_piece.shape[1])
    kv_width = KVH * HD
    keys_part = kv_piece[:, :, :kv_width].reshape(seq_count, row_count, KVH, HD)
    values_part = kv_piece[:, :, kv_width:].reshape(seq_count, row_count, KVH, HD)
    return (keys_part, values_part)


def scores_of(queries, keys_part, query_pos, key_pos):
    raw_scores = jnp.einsum(
        "skgqd,stkd->skgqt", queries, keys_part, preferred_element_type=jnp.float32
    ) * HD ** (-0.5)
    allowed = key_pos[None, :] <= query_pos[:, None]
    return (raw_scores, allowed)


def forward_block(running, queries, query_pos, kv_piece, key_pos):
    row_max, row_sum, weighted = running
    keys_part, values_part = split_kv(kv_piece)
    raw_scores, allowed = scores_of(queries, keys_part, query_pos, key_pos)
    masked = jnp.where(allowed, raw_scores, FAR)
    new_max = jnp.maximum(row_max, jnp.max(masked, -1))
    exp_terms = jnp.where(allowed, jnp.exp(masked - new_max[..., None]), 0.0)
    factor = jnp.exp(row_max - new_max)
    row_sum = row_sum * factor + jnp.sum(exp_terms, -1)
    update = jnp.einsum(
        "skgqt,stkd->skgqd",
        exp_terms.astype(jnp.bfloat16),
        values_part,
        preferred_element_type=jnp.float32,
    )
    weighted = weighted * factor[..., None] + update
    return (new_max, row_sum, weighted)


def backward_block(queries, grads_out, log_norm, row_delta, query_pos, kv_piece, key_pos):
    keys_part, values_part = split_kv(kv_piece)
    raw_scores, allowed = scores_of(queries, keys_part, query_pos, key_pos)
    prob_full = jnp.where(allowed, jnp.exp(raw_scores - log_norm[..., None]), 0.0)
    dprobs = jnp.einsum(
        "skgqd,stkd->skgqt", grads_out, values_part, preferred_element_type=jnp.float32
    )
    dscores = (prob_full * (dprobs - row_delta[..., None])).astype(jnp.bfloat16)
    dquery = None
    dpiece = None
    dquery = jnp.einsum(
        "skgqt,stkd->skgqd", dscores, keys_part, preferred_element_type=jnp.float32
    ) * HD ** (-0.5)
    key_grads = jnp.einsum(
        "skgqt,skgqd->stkd", dscores, queries, preferred_element_type=jnp.float32
    ) * HD ** (-0.5)
    dvalues = jnp.einsum(
        "skgqt,skgqd->stkd",
        prob_full.astype(jnp.bfloat16),
        grads_out,
        preferred_element_type=jnp.float32,
    )
    seq_count, row_count = (kv_piece.shape[0], kv_piece.shape[1])
    dpiece = jnp.concatenate(
        [
            key_grads.reshape(seq_count, row_count, KVH * HD),
            dvalues.reshape(seq_count, row_count, KVH * HD),
        ],
        -1,
    )
    return (dquery, dpiece)


def block_loop(running, pieces, positions, step_fn, unit_rows):
    row_count = positions.shape[0]
    block_rows = math.gcd(row_count, unit_rows)
    block_count = row_count // block_rows
    stacked = tuple(
        (
            jnp.moveaxis(
                part_in.reshape(part_in.shape[:1] + (block_count, block_rows) + part_in.shape[2:]),
                1,
                0,
            )
            for part_in in pieces
        )
    )
    position_blocks = positions.reshape(block_count, block_rows)

    def block_advance(carried, scan_item):
        return (step_fn(carried, scan_item[0], scan_item[1]), None)

    result, unused = lax.scan(block_advance, running, (stacked, position_blocks))
    return result


def outer_sum(left, right):
    return lax.dot_general(
        left, right, (((0, 1), (0, 1)), ((), ())), preferred_element_type=jnp.float32
    )


def times_transposed(grad_in, weight):
    return lax.dot_general(
        grad_in, weight, (((2,), (1,)), ((), ())), preferred_element_type=jnp.float32
    )


def body(
    layer_input,
    out_grad,
    attn_gain,
    w_query,
    w_key,
    w_value,
    w_output,
    mlp_gain,
    w_gate,
    w_up,
    w_down,
):
    gain_one, query_all, key_all, value_all, output_all = (
        lax.all_gather(attn_gain, "fsdp", axis=0, tiled=True),
        lax.all_gather(w_query, "fsdp", axis=0, tiled=True),
        lax.all_gather(w_key, "fsdp", axis=0, tiled=True),
        lax.all_gather(w_value, "fsdp", axis=0, tiled=True),
        lax.all_gather(w_output, "fsdp", axis=0, tiled=True),
    )
    gain_two, gate_all, up_all, down_all = (
        lax.all_gather(mlp_gain, "fsdp", axis=0, tiled=True),
        lax.all_gather(w_gate, "fsdp", axis=0, tiled=True),
        lax.all_gather(w_up, "fsdp", axis=0, tiled=True),
        lax.all_gather(w_down, "fsdp", axis=0, tiled=True),
    )
    seq_count, shard_rows = (layer_input.shape[0], layer_input.shape[1])
    ctx_size = lax.axis_size("ctx")
    ctx_index = lax.axis_index("ctx")
    local_pos = place_rows(ctx_index * shard_rows, shard_rows, shard_rows, ctx_size)
    unit_rows = 4 * shard_rows
    group_size = QH // KVH
    head_shape = (seq_count, KVH, group_size, shard_rows)
    source = layer_input.astype(jnp.float32)
    inv_one = lax.rsqrt(jnp.mean(source * source, -1, keepdims=True) + EPS)
    normed_one = source * inv_one
    gain_first = gain_one.astype(jnp.float32)
    h_one = (normed_one * gain_first).astype(jnp.bfloat16)
    queries_flat = rotate(
        jnp.dot(h_one, query_all, preferred_element_type=jnp.float32), local_pos, QH, 1.0
    ).astype(jnp.bfloat16)
    keys_flat = rotate(
        jnp.dot(h_one, key_all, preferred_element_type=jnp.float32), local_pos, KVH, 1.0
    ).astype(jnp.bfloat16)
    values_flat = jnp.dot(h_one, value_all, preferred_element_type=jnp.float32).astype(jnp.bfloat16)
    kv_local = jnp.concatenate([keys_flat, values_flat], -1)
    q_heads = to_heads(queries_flat)
    start_state = (
        jnp.full(head_shape, FAR, jnp.float32),
        jnp.zeros(head_shape, jnp.float32),
        jnp.zeros(head_shape + (HD,), jnp.float32),
    )
    kv_piece = lax.all_gather(kv_local, "ctx", axis=1, tiled=True)
    key_pos = place_rows(jnp.int32(0), kv_piece.shape[1], shard_rows, ctx_size)

    def step_fn(carried, blocks, positions):
        return forward_block(carried, q_heads, local_pos, blocks[0], positions)

    row_max, row_sum, weighted = block_loop(start_state, (kv_piece,), key_pos, step_fn, unit_rows)
    attended_full = weighted / row_sum[..., None]
    log_norm = row_max + jnp.log(row_sum)
    attended = from_heads(attended_full).astype(jnp.bfloat16)
    middle = source + jnp.dot(attended, output_all, preferred_element_type=jnp.float32)
    inv_two = lax.rsqrt(jnp.mean(middle * middle, -1, keepdims=True) + EPS)
    normed_two = middle * inv_two
    gain_mid = gain_two.astype(jnp.float32)
    h_two = (normed_two * gain_mid).astype(jnp.bfloat16)
    gate = jnp.dot(h_two, gate_all, preferred_element_type=jnp.float32)
    up_proj = jnp.dot(h_two, up_all, preferred_element_type=jnp.float32)
    sigma = jax.nn.sigmoid(gate)
    silu_gate = gate * sigma
    hidden = (silu_gate * up_proj).astype(jnp.bfloat16)
    layer_output = (middle + jnp.dot(hidden, down_all, preferred_element_type=jnp.float32)).astype(
        jnp.bfloat16
    )
    g_hidden = times_transposed(out_grad, down_all)
    down_grad = outer_sum(hidden, out_grad)
    gate_slope = sigma * (1.0 + gate * (1.0 - sigma))
    g_gate = (g_hidden * up_proj * gate_slope).astype(jnp.bfloat16)
    g_up = (g_hidden * silu_gate).astype(jnp.bfloat16)
    gate_grad = outer_sum(h_two, g_gate)
    up_grad = outer_sum(h_two, g_up)
    g_h_two = times_transposed(g_gate, gate_all) + times_transposed(g_up, up_all)
    mlp_gain_grad = jnp.sum(g_h_two * normed_two, (0, 1))
    g_normed_two = g_h_two * gain_mid
    g_middle = out_grad.astype(jnp.float32) + inv_two * (
        g_normed_two - normed_two * jnp.mean(g_normed_two * normed_two, -1, keepdims=True)
    )
    g_branch = g_middle.astype(jnp.bfloat16)
    output_grad = outer_sum(attended, g_branch)
    g_attended = times_transposed(g_branch, output_all).astype(jnp.bfloat16)
    grad_heads = to_heads(g_attended)
    row_delta = jnp.sum(grad_heads.astype(jnp.float32) * attended_full, -1)
    everything = lax.all_gather(kv_local, "ctx", axis=1, tiled=True)
    total_rows = everything.shape[1]
    block_rows = math.gcd(total_rows, unit_rows)
    block_count = total_rows // block_rows
    kv_blocks = jnp.moveaxis(
        everything.reshape(seq_count, block_count, block_rows, everything.shape[2]), 1, 0
    )
    key_blocks = place_rows(0, total_rows, shard_rows, ctx_size).reshape(block_count, block_rows)

    def body_advance(dquery, scan_item):
        part_query, part_kv = backward_block(
            q_heads, grad_heads, log_norm, row_delta, local_pos, scan_item[0], scan_item[1]
        )
        return (dquery + part_query, part_kv)

    dquery, kv_terms = lax.scan(
        body_advance, jnp.zeros(head_shape + (HD,), jnp.float32), (kv_blocks, key_blocks)
    )
    kv_term = jnp.moveaxis(kv_terms, 0, 1).reshape(seq_count, total_rows, kv_terms.shape[-1])
    kv_grad = lax.psum_scatter(
        kv_term.astype(jnp.bfloat16), "ctx", scatter_dimension=1, tiled=True
    ).astype(jnp.float32)
    kv_width = KVH * HD
    g_query_proj = rotate(from_heads(dquery), local_pos, QH, -1.0).astype(jnp.bfloat16)
    g_key_proj = rotate(kv_grad[:, :, :kv_width], local_pos, KVH, -1.0).astype(jnp.bfloat16)
    g_value_proj = kv_grad[:, :, kv_width:].astype(jnp.bfloat16)
    query_grad = outer_sum(h_one, g_query_proj)
    key_grad = outer_sum(h_one, g_key_proj)
    value_grad = outer_sum(h_one, g_value_proj)
    g_h_one = (
        times_transposed(g_query_proj, query_all)
        + times_transposed(g_key_proj, key_all)
        + times_transposed(g_value_proj, value_all)
    )
    attn_gain_grad = jnp.sum(g_h_one * normed_one, (0, 1))
    g_normed_one = g_h_one * gain_first
    input_grad = (
        g_middle
        + inv_one
        * (g_normed_one - normed_one * jnp.mean(g_normed_one * normed_one, -1, keepdims=True))
    ).astype(jnp.bfloat16)
    shards = (
        lax.psum_scatter(
            attn_gain_grad.astype(jnp.bfloat16), "fsdp", scatter_dimension=0, tiled=True
        ).astype(jnp.float32),
        lax.psum_scatter(
            query_grad.astype(jnp.bfloat16), "fsdp", scatter_dimension=0, tiled=True
        ).astype(jnp.float32),
        lax.psum_scatter(
            key_grad.astype(jnp.bfloat16), "fsdp", scatter_dimension=0, tiled=True
        ).astype(jnp.float32),
        lax.psum_scatter(
            value_grad.astype(jnp.bfloat16), "fsdp", scatter_dimension=0, tiled=True
        ).astype(jnp.float32),
        lax.psum_scatter(
            output_grad.astype(jnp.bfloat16), "fsdp", scatter_dimension=0, tiled=True
        ).astype(jnp.float32),
        lax.psum_scatter(
            mlp_gain_grad.astype(jnp.bfloat16), "fsdp", scatter_dimension=0, tiled=True
        ).astype(jnp.float32),
        lax.psum_scatter(
            gate_grad.astype(jnp.bfloat16), "fsdp", scatter_dimension=0, tiled=True
        ).astype(jnp.float32),
        lax.psum_scatter(
            up_grad.astype(jnp.bfloat16), "fsdp", scatter_dimension=0, tiled=True
        ).astype(jnp.float32),
        lax.psum_scatter(
            down_grad.astype(jnp.bfloat16), "fsdp", scatter_dimension=0, tiled=True
        ).astype(jnp.float32),
    )
    summed = (
        lax.psum(shards[0].astype(jnp.bfloat16), "ctx").astype(jnp.float32),
        lax.psum(shards[1].astype(jnp.bfloat16), "ctx").astype(jnp.float32),
        lax.psum(shards[2].astype(jnp.bfloat16), "ctx").astype(jnp.float32),
        lax.psum(shards[3].astype(jnp.bfloat16), "ctx").astype(jnp.float32),
        lax.psum(shards[4].astype(jnp.bfloat16), "ctx").astype(jnp.float32),
        lax.psum(shards[5].astype(jnp.bfloat16), "ctx").astype(jnp.float32),
        lax.psum(shards[6].astype(jnp.bfloat16), "ctx").astype(jnp.float32),
        lax.psum(shards[7].astype(jnp.bfloat16), "ctx").astype(jnp.float32),
        lax.psum(shards[8].astype(jnp.bfloat16), "ctx").astype(jnp.float32),
    )
    return (layer_output, input_grad) + tuple(summed)


def solution(mesh):
    in_specs = (
        P("fsdp", "ctx", None),
        P("fsdp", "ctx", None),
        P("fsdp"),
        P("fsdp", None),
        P("fsdp", None),
        P("fsdp", None),
        P("fsdp", None),
        P("fsdp"),
        P("fsdp", None),
        P("fsdp", None),
        P("fsdp", None),
    )
    out_specs = (
        P("fsdp", "ctx", None),
        P("fsdp", "ctx", None),
        P("fsdp"),
        P("fsdp", None),
        P("fsdp", None),
        P("fsdp", None),
        P("fsdp", None),
        P("fsdp"),
        P("fsdp", None),
        P("fsdp", None),
        P("fsdp", None),
    )
    return jax.shard_map(body, mesh=mesh, in_specs=in_specs, out_specs=out_specs, check_vma=False)
```

profile of v0, /device:TPU:1, one launch (start us, length us, event | category | flops | bytes accessed | tf_op | source)
XLA Modules:
  0.0 1216.4 jit_solution(1366772254119476833)
XLA Ops:
  25.7 15.8 %all-gather.1 = bf16[2,480,320]{1,2,0:T(8,128)(2,1)S(1)} all-gather(bf16[1,480,320]{1,2,0:T(8,128)(2,1)S(1)} %bitcast.331), channel_id=1, replica_groups=mesh['ctx'=16,'fsdp'=2] {'fsdp'}, dimensions={0}, use_global_device_ids=true | all-gather | bytes 921600 | tf_op jit(solution)/shard_map/all_gather | solution.py:170
  58.0 63.3 %all-gather.19.cloned.1.call-done = bf16[2560,960]{0,1:T(8,128)(2,1)} async-done(((bf16[1280,960]{0,1:T(8,128)(2,1)}), bf16[2560,960]{0,1:T(8,128)(2,1)}) %all-gather.19.cloned.1.call-update) | async-done | bytes 4915216 | tf_op jit(solution)/shard_map/all_gather | solution.py:177
  128.9 86.4 %all-gather.9.cloned.1.call-done = bf16[4,2048,640]{1,2,0:T(8,128)(2,1)} async-done(((bf16[4,128,640]{1,2,0:T(8,128)(2,1)}), bf16[4,2048,640]{1,2,0:T(8,128)(2,1)}) %all-gather.9.cloned.1.call-update) | async-done | bytes 10485776 | tf_op jit(solution)/shard_map/all_gather | solution.py:205
  224.8 114.5 %while.28 = (s32[]{:T(128)}, f32[4,5,3,128]{3,2,1,0:T(4,128)S(1)}, f32[4,5,3,128]{3,2,1,0:T(4,128)S(1)}, f32[4,5,3,128,64]{3,4,2,1,0:T(8,128)}, s32[4,512]{1,0:T...) while((s32[]{:T(128)}, f32[4,5,3,128]{3,2,1,0:T(4,128)S(1)}, ...), condition=%wide.region_4.5_spmd.clone, body=%wide.region_1.4_spmd.clone.sunk | while | flops 1059333120 | bytes 81697968 | solution.py:137
  233.8 9.9 fusion.163
  262.9 9.9 fusion.163
  290.8 9.9 fusion.163
  318.7 11.6 fusion.163
  353.2 25.5 %all-gather.15.cloned.1.call-done = bf16[960,2560]{1,0:T(8,128)(2,1)} async-done(((bf16[480,2560]{1,0:T(8,128)(2,1)}), bf16[960,2560]{1,0:T(8,128)(2,1)}) %all-gather.15.cloned.1.call-update) | async-done | bytes 4915216 | tf_op jit(solution)/shard_map/all_gather | solution.py:175
  378.7 10.5 multiply_convert_fusion.1
  402.2 141.1 %while.29 = (s32[]{:T(128)}, f32[4,5,3,128,64]{3,4,2,1,0:T(8,128)}, bf16[4,4,512,640]{2,3,1,0:T(8,128)(2,1)}, s32[4,512]{1,0:T(4,128)S(1)}, bf16[4,4,512,640]{2,...) while((s32[]{:T(128)}, f32[4,5,3,128,64]{3,4,2,1,0:T(8,128)}, ...), condition=%wide.region_9.10_spmd.clone, body=%wide.region_8.9_spmd.clone.sunk | while | flops 2564001280 | bytes 130057504 | solution.py:261
  413.2 9.8 fusion.179
  448.4 9.8 fusion.179
  483.6 9.8 fusion.179
  543.3 16.9 %copy.64 = bf16[4,4,512,640]{3,0,2,1:T(4,128)(2,1)} copy(bf16[4,4,512,640]{2,3,0,1:T(8,128)(2,1)} %bitcast.311) | data formatting | bytes 20971520
  560.1 9.9 copy.69
  570.1 119.1 %reduce-scatter.25.cloned.1.call-done = bf16[128,2560]{1,0:T(8,128)(2,1)} async-done(((bf16[2048,2560]{1,0:T(8,128)(2,1)}), bf16[128,2560]{1,0:T(8,128)(2,1)}) %reduce-scatter.25.cloned.1.call-update) | async-done | bytes 655376
  734.3 29.4 %reduce-scatter.17.cloned.1.call-done = bf16[480,960]{1,0:T(8,128)(2,1)} async-done(((bf16[960,960]{1,0:T(8,128)(2,1)}), bf16[480,960]{1,0:T(8,128)(2,1)}) %reduce-scatter.17.cloned.1.call-update) | async-done | bytes 921616 | tf_op jit(solution)/shard_map/reduce_scatter | solution.py:300
  763.7 33.4 %reduce-scatter.15.cloned.1.call-done = bf16[480,960]{1,0:T(8,128)(2,1)} async-done(((bf16[960,960]{1,0:T(8,128)(2,1)}), bf16[480,960]{1,0:T(8,128)(2,1)}) %reduce-scatter.15.cloned.1.call-update) | async-done | bytes 921616 | tf_op jit(solution)/shard_map/reduce_scatter | solution.py:291
  797.1 64.9 %reduce-scatter.23.cloned.1.call-done = bf16[1280,960]{0,1:T(8,128)(2,1)} async-done(((bf16[2560,960]{0,1:T(8,128)(2,1)}), bf16[1280,960]{0,1:T(8,128)(2,1)}) %reduce-scatter.23.cloned.1.call-update) | async-done | bytes 2457616 | tf_op jit(solution)/shard_map/reduce_scatter | solution.py:312
  862.0 65.1 %reduce-scatter.19.cloned.1.call-done = bf16[480,2560]{1,0:T(8,128)(2,1)} async-done(((bf16[960,2560]{1,0:T(8,128)(2,1)}), bf16[480,2560]{1,0:T(8,128)(2,1)}) %reduce-scatter.19.cloned.1.call-update) | async-done | bytes 2457616 | tf_op jit(solution)/shard_map/reduce_scatter | solution.py:306
  927.0 64.9 %reduce-scatter.21.cloned.1.call-done = bf16[480,2560]{1,0:T(8,128)(2,1)} async-done(((bf16[960,2560]{1,0:T(8,128)(2,1)}), bf16[480,2560]{1,0:T(8,128)(2,1)}) %reduce-scatter.21.cloned.1.call-update) | async-done | bytes 2457616 | tf_op jit(solution)/shard_map/reduce_scatter | solution.py:309
  1008.5 32.1 %all-reduce.4 = (bf16[480]{0:T(512)(128)(2,1)S(1)}, bf16[480]{0:T(512)(128)(2,1)S(1)}) all-reduce(bf16[480]{0:T(512)(128)(2,1)S(1)} %dynamic-slice.3, bf16[480]{0:T(512)(128)(2,1)S(1)} %dynamic-slice.5), channel_id=1, replica_groups=mesh['ctx'=16,'fsdp'=2] {'ctx'}, use_global_device_ids=true, to_apply=%region_14.15 | all-reduce | flops 960 | bytes 3840 | tf_op jit(solution)/shard_map/psum | solution.py:317
  1044.8 148.6 %all-reduce.10.cloned.1.call-done = (bf16[480,960]{1,0:T(8,128)(2,1)}, bf16[480,320]{0,1:T(8,128)(2,1)}, bf16[480,320]{0,1:T(8,128)(2,1)}, bf16[480,960]{1,0:T(8...) async-done(((bf16[480,960]{1,0:T(8,128)(2,1)}, bf16[480,320]{0,1:T(8,128)(2,1)}, bf16[480,320]{0,1:T(8,128)(2,1)}, ...) | async-done | bytes 9830416 | tf_op jit(solution)/shard_map/psum | solution.py:318
  (366 shorter events, 342.9 us)
Async XLA Ops:
  7.2 46.4 %all-gather.11.cloned.1.call-start = ((), (), s32[]{:S(2)}) async-start(), calls=%async_computation.9 | async-start | bytes 2949120 | tf_op jit(solution)/shard_map/all_gather | solution.py:168
  8.0 113.4 %all-gather.19.cloned.1.call-start = ((), (), s32[]{:S(2)}) async-start(), calls=%async_computation.13 | async-start | bytes 7372800 | tf_op jit(solution)/shard_map/all_gather | solution.py:177
  8.7 17.0 %copy-start.41 = (bf16[480,320]{0,1:T(8,128)(2,1)S(1)}, bf16[480,320]{0,1:T(8,128)(2,1)}, u32[]{:S(2)}) copy-start(bf16[480,320]{0,1:T(8,128)(2,1)} %param.20) | copy-start | bytes 921604
  8.7 206.6 %all-gather.9.cloned.1.call-start = ((), (), s32[]{:S(2)}) async-start(), calls=%async_computation.8 | async-start | bytes 11141120 | tf_op jit(solution)/shard_map/all_gather | solution.py:205
  14.9 38.7 %copy-start.43 = (f32[960]{0:T(1024)}, f32[960]{0:T(1024)S(1)}, u32[]{:S(2)}) copy-start(f32[960]{0:T(1024)S(1)} %convert_element_type.169) | copy-start | bytes 11524
  25.6 18.2 %copy-start.24 = (bf16[960,320,1]{0,1,2:T(8,128)(2,1)}, bf16[960,320,1]{0,1,2:T(8,128)(2,1)S(1)}, u32[]{:S(2)}) copy-start(bf16[960,320,1]{0,1,2:T(8,128)(2,1)S(1)} %reshape.237) | copy-start | bytes 1843204
  25.6 18.0 %copy-start.4 = (bf16[4,128,960]{1,2,0:T(8,128)(2,1)S(1)}, bf16[4,128,960]{1,2,0:T(8,128)(2,1)}, u32[]{:S(2)}) copy-start(bf16[4,128,960]{1,2,0:T(8,128)(2,1)} %param.15) | copy-start | bytes 2949124
  46.3 294.9 %all-gather.13.cloned.1.call-start = ((), (), s32[]{:S(2)}) async-start(), calls=%async_computation.10 | async-start | bytes 2949120 | tf_op jit(solution)/shard_map/all_gather | solution.py:171
  46.9 299.0 %all-gather.17.cloned.1.call-start = ((), (), s32[]{:S(2)}) async-start(), calls=%async_computation.12 | async-start | bytes 7372800 | tf_op jit(solution)/shard_map/all_gather | solution.py:176
  47.4 331.3 %all-gather.15.cloned.1.call-start = ((), (), s32[]{:S(2)}) async-start(), calls=%async_computation.11 | async-start | bytes 7372800 | tf_op jit(solution)/shard_map/all_gather | solution.py:175
  48.0 641.1 %reduce-scatter.25.cloned.1.call-start = ((), (), s32[]{:S(2)}) async-start(), calls=%async_computation.19 | async-start | bytes 11141120
  57.8 63.6 %copy-start.17 = (bf16[4,128,960]{1,2,0:T(8,128)(2,1)S(1)}, bf16[4,128,960]{1,2,0:T(8,128)(2,1)}, u32[]{:S(2)}) copy-start(bf16[4,128,960]{1,2,0:T(8,128)(2,1)} %param.16) | copy-start | bytes 2949124
  233.8 10.0 copy-start.6
  318.7 11.7 copy-start.6
  345.8 32.9 %copy-start.20 = (bf16[4,128,960]{1,2,0:T(8,128)(2,1)}, bf16[4,128,960]{1,2,0:T(8,128)(2,1)S(1)}, u32[]{:S(2)}) copy-start(bf16[4,128,960]{1,2,0:T(8,128)(2,1)S(1)} %multiply_convert_fusion.3) | copy-start | bytes 2949124
  378.7 10.5 copy-start.14
  570.0 160.6 %reduce-scatter.27.cloned.1.call-start = ((), (), s32[]{:S(2)}) async-start(), calls=%async_computation.20 | async-start | bytes 1105920
  695.1 37.4 %reduce-scatter.29.cloned.1.call-start = ((), (), s32[]{:S(2)}) async-start(), calls=%async_computation.21 | async-start | bytes 1105920
  699.2 64.5 %reduce-scatter.17.cloned.1.call-start = ((), (), s32[]{:S(2)}) async-start(), calls=%async_computation.15 | async-start | bytes 2949120 | tf_op jit(solution)/shard_map/reduce_scatter | solution.py:300
  703.0 94.0 %reduce-scatter.15.cloned.1.call-start = ((), (), s32[]{:S(2)}) async-start(), calls=%async_computation.14 | async-start | bytes 2949120 | tf_op jit(solution)/shard_map/reduce_scatter | solution.py:291
  709.7 152.3 %reduce-scatter.23.cloned.1.call-start = ((), (), s32[]{:S(2)}) async-start(), calls=%async_computation.18 | async-start | bytes 7372800 | tf_op jit(solution)/shard_map/reduce_scatter | solution.py:312
  717.0 210.0 %reduce-scatter.19.cloned.1.call-start = ((), (), s32[]{:S(2)}) async-start(), calls=%async_computation.16 | async-start | bytes 7372800 | tf_op jit(solution)/shard_map/reduce_scatter | solution.py:306
  724.3 267.6 %reduce-scatter.21.cloned.1.call-start = ((), (), s32[]{:S(2)}) async-start(), calls=%async_computation.17 | async-start | bytes 7372800 | tf_op jit(solution)/shard_map/reduce_scatter | solution.py:309
  730.5 462.9 %all-reduce.10.cloned.1.call-start = ((), (), s32[]{:S(2)}) async-start(), calls=%async_computation.22 | async-start | bytes 19988480 | tf_op jit(solution)/shard_map/psum | solution.py:318
  (68 other events, 199.9 us)
Sparse Core Ops, SparseCore 0:
  9.6 43.9 all-gather.10
  55.2 66.1 all-gather.18
  124.1 91.1 all-gather.8
  216.7 29.3 all-gather.12
  247.5 64.8 all-gather.16
  313.8 64.8 all-gather.14
  570.1 118.9 reduce-scatter.24
  695.2 16.7 reduce-scatter.26
  714.3 16.8 reduce-scatter.28
  733.3 30.3 reduce-scatter.16
  766.6 30.3 reduce-scatter.14
  799.8 62.0 reduce-scatter.22
  864.9 62.1 reduce-scatter.18
  929.8 62.1 reduce-scatter.20
  997.1 196.2 all-reduce.9
where the time goes:
time: 1220 us
  waiting for transfers between devices  709 us (58%)
  matrix products  253 us (21%)
  local copies, waits for them, and re-layouts  94.5 us (8%)
  other arithmetic  76.1 us (6%)
  blocking collectives  65.9 us (5%)
  between operations  16.2 us (1%)
    psum x1, waiting for transfers between devices, body(): lax.psum(shards[1].astype(jnp.bfloat16), 'ctx').astype(jnp.float32)  149 us
    unnamed x18, waiting for transfers between devices  122 us
    all_gather x1, waiting for transfers between devices, body(): kv_piece = lax.all_gather(kv_local, 'ctx', axis=1, tiled=True)  86.4 us
    reduce_scatter x1, waiting for transfers between devices, body(): lax.psum_scatter(gate_grad.astype(jnp.bfloat16), 'fsdp', scatter_dimensio...  65.1 us
    reduce_scatter x1, waiting for transfers between devices, body(): lax.psum_scatter(up_grad.astype(jnp.bfloat16), 'fsdp', scatter_dimension=...  64.9 us
    reduce_scatter x1, waiting for transfers between devices, body(): lax.psum_scatter(down_grad.astype(jnp.bfloat16), 'fsdp', scatter_dimensio...  64.9 us
    all_gather x1, waiting for transfers between devices, body(): lax.all_gather(w_down, 'fsdp', axis=0, tiled=True)  63.3 us
    dot_general x8, matrix products, scores_of(): jnp.einsum('skgqd,stkd->skgqt', queries, keys_part, preferred_element_typ...  54.2 us
  transfers between devices with their start and end apart: 15, of which 11 were waited for; matrix products, arithmetic and copies ran while one was open for 16% of the time, Pallas kernels for 0%

commit v1 on v0

v1 whole, which is shorter than its diff:
```python
import jax
import jax.numpy as jnp
from jax import lax
from jax.experimental import pallas as pl
from jax.experimental.pallas import tpu as pltpu
from jax.sharding import PartitionSpec as P

QH = 15
KVH = 5
HD = 64
GROUP = QH // KVH


EPS = 1e-05
THETA = 100000.0
FAR = -1e30


def place_rows(start_row, row_count, shard_rows, ctx_size):
    stored = start_row + jnp.arange(row_count, dtype=jnp.int32)
    half_rows = shard_rows // 2
    holder = stored // shard_rows
    within = stored % shard_rows
    mirror = (2 * ctx_size - 1 - holder) * half_rows + within - half_rows
    return jnp.where(within < half_rows, holder * half_rows + within, mirror)


def rotate(values_in, position, heads, sign):
    full_shape = values_in.shape
    by_head = values_in.reshape(full_shape[:-1] + (heads, HD))
    frequency = THETA ** (-jnp.arange(0, HD, 2, dtype=jnp.float32) / HD)
    angles = position.astype(jnp.float32)[:, None] * frequency[None, :]
    cosine = jnp.concatenate([jnp.cos(angles), jnp.cos(angles)], -1)[:, None, :]
    sine_part = sign * jnp.concatenate([jnp.sin(angles), jnp.sin(angles)], -1)[:, None, :]
    first_half = by_head[..., : HD // 2]
    second_half = by_head[..., HD // 2 :]
    turned = jnp.concatenate([-second_half, first_half], -1)
    return (by_head * cosine + turned * sine_part).reshape(full_shape)


def outer_sum(left, right):
    return lax.dot_general(
        left, right, (((0, 1), (0, 1)), ((), ())), preferred_element_type=jnp.float32
    )


def times_transposed(grad_in, weight):
    return lax.dot_general(
        grad_in, weight, (((2,), (1,)), ((), ())), preferred_element_type=jnp.float32
    )


def fsdp_gather(shard, half_of_core):
    if lax.axis_size("fsdp") != 2 or lax.axis_size("ctx") % 2:
        return lax.all_gather(shard, "fsdp", axis=0, tiled=True)
    f = lax.axis_index("fsdp")
    rows = shard.shape[0]
    half = rows // 2
    piece = lax.dynamic_slice_in_dim(shard, half_of_core * half, half, 0)
    got = lax.ppermute(piece, "fsdp", [(0, 1), (1, 0)])
    other = xor_permute(got, 1)
    full = jnp.zeros((2 * rows,) + shard.shape[1:], shard.dtype)
    full = lax.dynamic_update_slice_in_dim(full, shard, f * rows, 0)
    start = (1 - f) * rows
    full = lax.dynamic_update_slice_in_dim(full, got, start + half_of_core * half, 0)
    return lax.dynamic_update_slice_in_dim(full, other, start + (1 - half_of_core) * half, 0)


def xor_permute(array, mask):
    size = lax.axis_size("ctx")
    return lax.ppermute(array, "ctx", [(i, i ^ mask) for i in range(size)])


def add_low(kept, received):
    total = kept.astype(jnp.float32) + received.astype(jnp.float32)
    return total.astype(jnp.bfloat16)


def reduce_grad(grad, split_dim):
    grad = grad.astype(jnp.bfloat16)
    size = lax.axis_size("ctx")
    if lax.axis_size("fsdp") != 2 or size & (size - 1) or size < 4:
        part = lax.psum_scatter(grad, "fsdp", scatter_dimension=0, tiled=True)
        return lax.psum(part, "ctx").astype(jnp.float32)
    f = lax.axis_index("fsdp")
    c = lax.axis_index("ctx")
    core = c & 1
    rows, cols = grad.shape
    parts = grad.reshape(2, 2, rows // 4, cols)
    keep = lax.dynamic_index_in_dim(parts, core, 1, False)
    send = lax.dynamic_index_in_dim(parts, 1 - core, 1, False)
    total = add_low(keep, xor_permute(send, 1))
    keep = lax.dynamic_index_in_dim(total, f, 0, False)
    send = lax.dynamic_index_in_dim(total, 1 - f, 0, False)
    total = add_low(keep, lax.ppermute(send, "fsdp", [(0, 1), (1, 0)]))
    masks = []
    mask = 2
    while mask < size:
        masks.append(mask)
        mask *= 2
    for mask in masks[:-1]:
        bit = (c // mask) % 2
        half = total.shape[split_dim] // 2
        keep = lax.dynamic_slice_in_dim(total, bit * half, half, split_dim)
        send = lax.dynamic_slice_in_dim(total, (1 - bit) * half, half, split_dim)
        total = add_low(keep, xor_permute(send, mask))
    total = add_low(total, xor_permute(total, masks[-1]))
    for mask in masks[:-1][::-1]:
        total = join(total, xor_permute(total, mask), (c // mask) % 2, split_dim)
    return join(total, xor_permute(total, 1), core, 0).astype(jnp.float32)


def join(mine, theirs, bit, dim):
    first = jnp.where(bit == 0, mine, theirs)
    second = jnp.where(bit == 0, theirs, mine)
    return jnp.concatenate([first, second], dim)


def gather_order(size, which):
    masks = []
    mask = size // 2
    while mask:
        masks.append(mask)
        mask //= 2
    if which % 2 and len(masks) >= 4:
        masks[1:3] = masks[1:3][::-1]
    return masks


def holders(size, masks):
    offsets = [0]
    for mask in masks:
        offsets = offsets + [offset ^ mask for offset in offsets]
    return jnp.array(offsets, jnp.int32)


def block_parts(kv, pick):
    slots = kv.shape[0] // (4 * HD) * 2
    split = kv.reshape(slots, 2, HD, 2 * HD)
    low = split[:, 0].reshape(slots * HD, 2 * HD)
    high = split[:, 1].reshape(slots * HD, 2 * HD)
    nothing = jnp.zeros((slots * HD, HD), kv.dtype)
    nothing_own = jnp.zeros((2 * HD, HD), kv.dtype)
    rest = 1 - pick

    def of(at):
        lows, highs = low[:, at : at + HD], high[:, at : at + HD]
        return jnp.concatenate(
            [
                jnp.concatenate([lows, nothing], 1),
                jnp.concatenate([highs * pick, lows * rest], 1),
                jnp.concatenate([nothing_own, kv[: 2 * HD, at : at + HD]], 1),
            ],
            0,
        )

    return of(0), of(HD)


def masked_scores(queries, keys, bias, wide):
    scores = lax.dot_general(
        queries, keys, (((1,), (1,)), ((), ())), preferred_element_type=jnp.float32
    )
    step = 2 * HD
    return jnp.concatenate(
        [
            scores[:, :wide],
            scores[:, wide : wide + step] + bias[:, :step],
            scores[:, wide + step : 2 * wide],
            scores[:, 2 * wide :] + bias[:, step:],
        ],
        1,
    )


def spread(high, low):
    shape = (high.shape[0], HD)
    return jnp.concatenate([jnp.broadcast_to(high, shape), jnp.broadcast_to(low, shape)], 1)


def forward_kernel(high_ref, pick_ref, bias_ref, q_ref, kv_ref, out_ref, norm_ref):
    wide = pick_ref.shape[0]
    keys, values = block_parts(kv_ref[...], pick_ref[...])
    scores = masked_scores(q_ref[0], keys, bias_ref[...], wide)
    is_high = high_ref[...] > 0.5
    high_max = jnp.max(jnp.where(is_high, scores, FAR), 1, keepdims=True)
    low_max = jnp.max(jnp.where(is_high, FAR, scores), 1, keepdims=True)
    terms = jnp.exp(scores - jnp.where(is_high, high_max, low_max))
    high_sum = jnp.sum(jnp.where(is_high, terms, 0.0), 1, keepdims=True)
    low_sum = jnp.sum(jnp.where(is_high, 0.0, terms), 1, keepdims=True)
    mixed = jnp.dot(terms.astype(jnp.bfloat16), values, preferred_element_type=jnp.float32)
    out_ref[0] = mixed / spread(high_sum, low_sum)
    norm_ref[0] = spread(high_max + jnp.log(high_sum), low_max + jnp.log(low_sum))


def backward_kernel(
    high_ref, pick_ref, bias_ref, q_ref, kv_ref, g_ref, out_ref, norm_ref, dq_ref, dkv_ref
):
    wide = pick_ref.shape[0]
    pick = pick_ref[...]
    queries, grads = q_ref[0], g_ref[0]
    keys, values = block_parts(kv_ref[...], pick)
    scores = masked_scores(queries, keys, bias_ref[...], wide)
    is_high = high_ref[...] > 0.5
    norm = norm_ref[0]
    probs = jnp.exp(scores - jnp.where(is_high, norm[:, :1], norm[:, HD : HD + 1]))
    product = grads.astype(jnp.float32) * out_ref[0]
    high_delta = jnp.sum(product[:, :HD], 1, keepdims=True)
    low_delta = jnp.sum(product[:, HD:], 1, keepdims=True)
    dprobs = lax.dot_general(
        grads, values, (((1,), (1,)), ((), ())), preferred_element_type=jnp.float32
    )
    dscores = (probs * (dprobs - jnp.where(is_high, high_delta, low_delta))).astype(jnp.bfloat16)
    dq_ref[0] = jnp.dot(dscores, keys, preferred_element_type=jnp.float32) * HD ** (-0.5)
    over_rows = (((0,), (0,)), ((), ()))
    dkeys = lax.dot_general(dscores, queries, over_rows, preferred_element_type=jnp.float32)
    dvalues = lax.dot_general(
        probs.astype(jnp.bfloat16), grads, over_rows, preferred_element_type=jnp.float32
    )
    pick_wide = pick.astype(jnp.float32)

    def fold(terms):
        low = terms[:wide, :HD] + terms[wide : 2 * wide, HD:] * (1.0 - pick_wide)
        own = low[:HD] + terms[2 * wide : 2 * wide + HD, HD:]
        return jnp.concatenate([own, low[HD:]], 0), terms[wide : 2 * wide, :HD] * pick_wide

    low_k, high_k = fold(dkeys)
    low_v, high_v = fold(dvalues)
    slots = wide // HD
    low = jnp.concatenate([low_k, low_v], 1).astype(jnp.bfloat16).reshape(slots, 1, HD, 2 * HD)
    high = jnp.concatenate([high_k, high_v], 1).astype(jnp.bfloat16).reshape(slots, 1, HD, 2 * HD)
    dkv_ref[...] = jnp.concatenate([low, high], 1).reshape(dkv_ref.shape)


def attention_call(kernel, consts, by_head, kv, backward):
    high_row, pick, bias = consts
    wide = pick.shape[0]
    rows = by_head[0].shape[1]
    whole = lambda array: pl.BlockSpec(array.shape, lambda g: (0, 0))
    head = pl.BlockSpec((1, rows, 2 * HD), lambda g: (g, 0, 0))
    kv_spec = pl.BlockSpec((kv.shape[0], 2 * HD), lambda g: (0, g))
    head_out = jax.ShapeDtypeStruct((KVH, rows, 2 * HD), jnp.float32)
    columns = 2 * wide + 2 * HD
    work = 2 * rows * columns * 2 * HD * KVH
    moved = KVH * rows * 2 * HD * 16 + kv.size * (4 if backward else 2)
    return pl.pallas_call(
        kernel,
        grid=(KVH,),
        in_specs=[whole(high_row), whole(pick), whole(bias), head, kv_spec]
        + [head] * (len(by_head) - 1),
        out_specs=[head, kv_spec if backward else head],
        out_shape=[head_out, jax.ShapeDtypeStruct(kv.shape, jnp.bfloat16) if backward else head_out],
        compiler_params=pltpu.CompilerParams(vmem_limit_bytes=52 * 1024 * 1024),
        cost_estimate=pl.CostEstimate(
            flops=work * (20 if backward else 8),
            bytes_accessed=moved,
            transcendentals=rows * columns * KVH,
        ),
    )(high_row, pick, bias, by_head[0], kv, *by_head[1:])


def stack_heads(flat):
    seqs = flat.shape[0]
    split = flat.reshape(seqs, 2, HD, KVH, GROUP, HD)[:, ::-1]
    return split.transpose(0, 3, 4, 2, 1, 5).reshape(seqs, KVH, GROUP * HD, 2 * HD)


def unstack_heads(stacked):
    seqs = stacked.shape[0]
    split = stacked.reshape(seqs, KVH, GROUP, HD, 2, HD).transpose(0, 4, 3, 1, 2, 5)[:, ::-1]
    return split.reshape(seqs, 2 * HD, QH * HD)


def body(
    layer_input,
    out_grad,
    attn_gain,
    w_query,
    w_key,
    w_value,
    w_output,
    mlp_gain,
    w_gate,
    w_up,
    w_down,
):
    size = lax.axis_size("ctx")
    c = lax.axis_index("ctx")
    core = c & 1
    q_width, kv_width = QH * HD, KVH * HD
    gains = jnp.stack([attn_gain, mlp_gain], 1)
    gains = jnp.pad(gains, ((0, 0), (0, HD - 2)))
    first_all = fsdp_gather(jnp.concatenate([w_query, w_key, w_value, gains], 1), core)
    output_all = fsdp_gather(w_output, core)
    gate_all = fsdp_gather(w_gate, core)
    up_all = fsdp_gather(w_up, core)
    down_all = fsdp_gather(w_down, core)
    proj_width = q_width + 2 * kv_width
    qkv_all = first_all[:, :proj_width]
    gain_first = first_all[:, proj_width].astype(jnp.float32)
    gain_mid = first_all[:, proj_width + 1].astype(jnp.float32)
    seq_count, shard_rows = (layer_input.shape[0], layer_input.shape[1])
    local_pos = place_rows(c * shard_rows, shard_rows, shard_rows, size)
    source = layer_input.astype(jnp.float32)
    inv_one = lax.rsqrt(jnp.mean(source * source, -1, keepdims=True) + EPS)
    normed_one = source * inv_one
    h_one = (normed_one * gain_first).astype(jnp.bfloat16)
    qkv = jnp.dot(h_one, qkv_all, preferred_element_type=jnp.float32)
    queries_flat = rotate(qkv[..., :q_width], local_pos, QH, 1.0).astype(jnp.bfloat16)
    keys_flat = rotate(qkv[..., q_width : q_width + kv_width], local_pos, KVH, 1.0)
    by_kv_head = (seq_count, shard_rows, KVH, HD)
    kv_local = jnp.concatenate(
        [
            keys_flat.astype(jnp.bfloat16).reshape(by_kv_head),
            qkv[..., q_width + kv_width :].astype(jnp.bfloat16).reshape(by_kv_head),
        ],
        -1,
    ).reshape(seq_count, shard_rows, 2 * kv_width)
    q_heads = stack_heads(queries_flat * jnp.bfloat16(HD ** (-0.5)))

    within = jnp.arange(GROUP * HD, dtype=jnp.int32)[:, None] % HD
    tile = jnp.arange(4 * HD, dtype=jnp.int32)[None, :]
    first_tile = (tile < HD) & (tile > within)
    spare_tile = (tile >= 2 * HD) & (tile - 2 * HD > within)
    bias = jnp.where(first_tile | spare_tile, FAR, 0.0).astype(jnp.float32)
    gathered, orders, consts = [], [], []
    for s in range(seq_count):
        masks = gather_order(size, s)
        pieces = kv_local[s]
        for mask in masks:
            pieces = jnp.concatenate([pieces, xor_permute(pieces, mask)], 0)
        picks = jnp.repeat((holders(size, masks) ^ c) >= c, HD)
        high_row = jnp.concatenate(
            [jnp.ones(size * HD, bool), picks, jnp.zeros(2 * HD, bool)]
        ).astype(jnp.float32)[None, :]
        pick = jnp.broadcast_to(picks[:, None], (size * HD, HD)).astype(jnp.bfloat16)
        gathered.append(pieces)
        orders.append(masks)
        consts.append((high_row, pick, bias))
    outs, norms = [], []
    for s in range(seq_count):
        out, norm = attention_call(forward_kernel, consts[s], (q_heads[s],), gathered[s], False)
        outs.append(out)
        norms.append(norm)
    attended = unstack_heads(jnp.stack(outs).astype(jnp.bfloat16))
    middle = source + jnp.dot(attended, output_all, preferred_element_type=jnp.float32)
    inv_two = lax.rsqrt(jnp.mean(middle * middle, -1, keepdims=True) + EPS)
    normed_two = middle * inv_two
    h_two = (normed_two * gain_mid).astype(jnp.bfloat16)
    gate = jnp.dot(h_two, gate_all, preferred_element_type=jnp.float32)
    up_proj = jnp.dot(h_two, up_all, preferred_element_type=jnp.float32)
    sigma = jax.nn.sigmoid(gate)
    silu_gate = gate * sigma
    hidden = (silu_gate * up_proj).astype(jnp.bfloat16)
    layer_output = (middle + jnp.dot(hidden, down_all, preferred_element_type=jnp.float32)).astype(
        jnp.bfloat16
    )
    g_hidden = times_transposed(out_grad, down_all)
    down_grad = outer_sum(hidden, out_grad)
    down_shard = reduce_grad(down_grad, 0)
    gate_slope = sigma * (1.0 + gate * (1.0 - sigma))
    g_gate = (g_hidden * up_proj * gate_slope).astype(jnp.bfloat16)
    g_up = (g_hidden * silu_gate).astype(jnp.bfloat16)
    gate_grad = outer_sum(h_two, g_gate)
    up_grad = outer_sum(h_two, g_up)
    gate_shard = reduce_grad(gate_grad, 1)
    up_shard = reduce_grad(up_grad, 1)
    g_h_two = times_transposed(g_gate, gate_all) + times_transposed(g_up, up_all)
    mlp_gain_grad = jnp.sum(g_h_two * normed_two, (0, 1))
    g_normed_two = g_h_two * gain_mid
    g_middle = out_grad.astype(jnp.float32) + inv_two * (
        g_normed_two - normed_two * jnp.mean(g_normed_two * normed_two, -1, keepdims=True)
    )
    g_branch = g_middle.astype(jnp.bfloat16)
    output_grad = outer_sum(attended, g_branch)
    output_shard = reduce_grad(output_grad, 0)
    g_attended = times_transposed(g_branch, output_all).astype(jnp.bfloat16)
    grad_heads = stack_heads(g_attended)
    dqueries, kv_grads = [], []
    for s in range(seq_count):
        dquery, term = attention_call(
            backward_kernel,
            consts[s],
            (q_heads[s], grad_heads[s], outs[s], norms[s]),
            gathered[s],
            True,
        )
        dqueries.append(dquery)
        for mask in orders[s][::-1]:
            half = term.shape[0] // 2
            term = add_low(term[:half], xor_permute(term[half:], mask))
        kv_grads.append(term)
    dquery_flat = unstack_heads(jnp.stack(dqueries))
    g_query_proj = rotate(dquery_flat, local_pos, QH, -1.0).astype(jnp.bfloat16)
    query_shard = reduce_grad(outer_sum(h_one, g_query_proj), 0)
    kv_grad = jnp.stack(kv_grads).reshape(seq_count, shard_rows, KVH, 2, HD)
    key_part = kv_grad[:, :, :, 0].reshape(seq_count, shard_rows, kv_width)
    g_key_proj = rotate(key_part.astype(jnp.float32), local_pos, KVH, -1.0).astype(jnp.bfloat16)
    g_value_proj = kv_grad[:, :, :, 1].reshape(seq_count, shard_rows, kv_width)
    g_kv = jnp.concatenate([g_key_proj, g_value_proj], -1)
    g_h_one = times_transposed(
        jnp.concatenate([g_query_proj, g_kv], -1), qkv_all
    )
    attn_gain_grad = jnp.sum(g_h_one * normed_one, (0, 1))
    gain_grads = jnp.pad(jnp.stack([attn_gain_grad, mlp_gain_grad], 1), ((0, 0), (0, HD - 2)))
    last_shard = reduce_grad(jnp.concatenate([outer_sum(h_one, g_kv), gain_grads], 1), 0)
    g_normed_one = g_h_one * gain_first
    input_grad = (
        g_middle
        + inv_one
        * (g_normed_one - normed_one * jnp.mean(g_normed_one * normed_one, -1, keepdims=True))
    ).astype(jnp.bfloat16)
    return (
        layer_output,
        input_grad,
        last_shard[:, 2 * kv_width],
        query_shard,
        last_shard[:, :kv_width],
        last_shard[:, kv_width : 2 * kv_width],
        output_shard,
        last_shard[:, 2 * kv_width + 1],
        gate_shard,
        up_shard,
        down_shard,
    )


def solution(mesh):
    in_specs = (
        P("fsdp", "ctx", None),
        P("fsdp", "ctx", None),
        P("fsdp"),
        P("fsdp", None),
        P("fsdp", None),
        P("fsdp", None),
        P("fsdp", None),
        P("fsdp"),
        P("fsdp", None),
        P("fsdp", None),
        P("fsdp", None),
    )
    out_specs = (
        P("fsdp", "ctx", None),
        P("fsdp", "ctx", None),
        P("fsdp"),
        P("fsdp", None),
        P("fsdp", None),
        P("fsdp", None),
        P("fsdp", None),
        P("fsdp"),
        P("fsdp", None),
        P("fsdp", None),
        P("fsdp", None),
    )
    return jax.shard_map(body, mesh=mesh, in_specs=in_specs, out_specs=out_specs, check_vma=False)
```

time: 1220 us -> 1050 us (0.86)
  waiting for transfers between devices: 709 us -> 375 us
  local copies, waits for them, and re-layouts: 94.5 us -> 292 us
  matrix products: 253 us -> 66.7 us
  starting transfers between devices: 0.6 us -> 116 us
  Pallas kernels: 0 us -> 90.7 us
  blocking collectives: 65.9 us -> 0 us
  other arithmetic: 76.1 us -> 90.6 us
  between operations: 16.2 us -> 3.56 us
    ppermute x0 -> x90, waiting for transfers between devices: none -> 375 us  [the longest x79 211 us: xor_permute(): return lax.ppermute(array, 'ctx', [(i, i ^ mask) for i in range(size)])]
    reduce_scatter x5 -> x0, waiting for transfers between devices: 258 us -> none  [the longest x1 65.1 us: body(): lax.psum_scatter(gate_grad.astype(jnp.bfloat16), 'fsdp', scatter_dimensio...]
    all_gather x6 -> x0, waiting for transfers between devices: 181 us -> none  [the longest x1 86.4 us: body(): kv_piece = lax.all_gather(kv_local, 'ctx', axis=1, tiled=True)]
    dot_general x31 -> x1, matrix products: 180 us -> 3.98 us  [body(): qkv = jnp.dot(h_one, qkv_all, preferred_element_type=jnp.float32)]
    psum x1 -> x0, waiting for transfers between devices: 149 us -> none  [body(): lax.psum(shards[1].astype(jnp.bfloat16), 'ctx').astype(jnp.float32)]
    unnamed x18 -> x0, waiting for transfers between devices: 122 us -> none
    ppermute x0 -> x90, starting transfers between devices: none -> 116 us  [the longest x79 106 us: xor_permute(): return lax.ppermute(array, 'ctx', [(i, i ^ mask) for i in range(size)])]
    pallas_call x0 -> x8, Pallas kernels: none -> 90.7 us  [attention_call(): pl.pallas_call(kernel, grid=(KVH,), in_specs=[whole(high_row), whole(pick...]
  transfers between devices with their start and end apart: 15 -> 90, of which waited for: 11 -> 42; matrix products, arithmetic and copies ran while one was open for 16% -> 22% of each run, Pallas kernels for 0% -> 2%
where the time goes in v1:
time: 1050 us; the launch traced here: 1030 us
  waiting for transfers between devices  375 us (36%)
  local copies, waits for them, and re-layouts  292 us (28%)
  starting transfers between devices  116 us (11%)
  Pallas kernels  90.7 us (9%)
  other arithmetic  90.6 us (9%)
  matrix products  66.7 us (6%)
    ppermute x79, waiting for transfers between devices, xor_permute(): return lax.ppermute(array, 'ctx', [(i, i ^ mask) for i in range(size)])  211 us
    ppermute x79, starting transfers between devices, xor_permute(): return lax.ppermute(array, 'ctx', [(i, i ^ mask) for i in range(size)])  106 us
    ppermute x6, waiting for transfers between devices, reduce_grad(): total = add_low(keep, lax.ppermute(send, 'fsdp', [(0, 1), (1, 0)]))  90.9 us
    pallas_call x8, Pallas kernels, attention_call(): pl.pallas_call(kernel, grid=(KVH,), in_specs=[whole(high_row), whole(pick...  90.7 us
    ppermute x5, waiting for transfers between devices, fsdp_gather(): got = lax.ppermute(piece, 'fsdp', [(0, 1), (1, 0)])  73.2 us
    rev x3, local copies, waits for them, and re-layouts, unstack_heads(): stacked.reshape(seqs, KVH, GROUP, HD, 2, HD).transpose(0, 4, 3, 1, 2, 5)  46.8 us
    unnamed x220, local copies, waits for them, and re-layouts  38.2 us
    rev x2, local copies, waits for them, and re-layouts, stack_heads(): split = flat.reshape(seqs, 2, HD, KVH, GROUP, HD)[:, ::-1]  36.8 us
  transfers between devices with their start and end apart: 90, of which 42 were waited for; matrix products, arithmetic and copies ran while one was open for 22% of the time, Pallas kernels for 2%

profile of v1, /device:TPU:1, one launch (start us, length us, event | category | flops | bytes accessed | tf_op | source)
XLA Modules:
  0.0 1034.5 jit_solution(741814428401434352)
XLA Ops:
  44.6 20.4 %collective-permute-done.24 = bf16[640,960]{0,1:T(8,128)(2,1)} collective-permute-done((bf16[640,960]{0,1:T(8,128)(2,1)}, bf16[640,960]{0,1:T(8,128)(2,1)}, u32[]{:S(2)}, u32[]{:S(2)}) %collective-permute-start.24) | collective-permute-done | bytes 1228832 | tf_op jit(solution)/shard_map/ppermute | solution.py:60
  67.0 24.3 %collective-permute-done.20 = bf16[240,2560]{1,0:T(8,128)(2,1)} collective-permute-done((bf16[240,2560]{1,0:T(8,128)(2,1)}, bf16[240,2560]{1,0:T(8,128)(2,1)}, u32[]{:S(2)}, u32[]{:S(2)}) %collective-permute-start.20) | collective-permute-done | bytes 1228832 | tf_op jit(solution)/shard_map/ppermute | solution.py:60
  93.3 24.3 %collective-permute-done.22 = bf16[240,2560]{1,0:T(8,128)(2,1)} collective-permute-done((bf16[240,2560]{1,0:T(8,128)(2,1)}, bf16[240,2560]{1,0:T(8,128)(2,1)}, u32[]{:S(2)}, u32[]{:S(2)}) %collective-permute-start.22) | collective-permute-done | bytes 1228832 | tf_op jit(solution)/shard_map/ppermute | solution.py:60
  150.9 17.8 %rev.12 = bf16[4,2,64,5,3,64]{5,1,2,4,3,0:T(2,128)(2,1)S(1)} reverse(bf16[4,2,64,5,3,64]{5,1,2,4,3,0:T(2,128)(2,1)} %copy.142), dimensions={1} | reverse | bytes 1966080 | tf_op jit(solution)/shard_map/rev | solution.py:264
  298.0 19.0 %rev.13 = bf16[4,2,64,5,3,64]{5,1,2,4,3,0:T(2,128)(2,1)} reverse(bf16[4,2,64,5,3,64]{5,1,2,4,3,0:T(2,128)(2,1)} %maximum_bitcast_fusion.1), dimensions={1} | reverse | bytes 1966080 | tf_op jit(solution)/shard_map/rev | solution.py:270
  371.4 19.0 %rev.14 = bf16[4,2,64,5,3,64]{5,1,2,4,3,0:T(2,128)(2,1)} reverse(bf16[4,2,64,5,3,64]{5,1,2,4,3,0:T(2,128)(2,1)} %copy.166), dimensions={1} | reverse | bytes 1966080 | tf_op jit(solution)/shard_map/rev | solution.py:264
  404.8 14.5 %shard_map.237 = (f32[5,192,128]{2,1,0:T(8,128)S(1)}, bf16[2048,640]{1,0:T(8,128)(2,1)}) custom-call(f32[1,2176]{1,0:T(1,128)S(1)} %get-tuple-element.131.high_ref, bf16[1024,64]{1,0:T(8,128)(2,1)S(1)} %broadcast_in_dim.46.pick_ref, f32[192,256]{1,0:T(8,128)S(1)} %copy-done.9, bf16[5,192,128]{2,1,0:T(8,128)(2,1)S(1)} %copy-done.3, ...), custom_call_target="tpu_custom_call" | custom-call | flops 10695475200 | bytes 7208960 | tf_op jit(solution)/shard_map/pallas_call | solution.py:246
  426.8 14.7 %shard_map.236 = (f32[5,192,128]{2,1,0:T(8,128)S(1)}, bf16[2048,640]{1,0:T(8,128)(2,1)}) custom-call(f32[1,2176]{1,0:T(1,128)S(1)} %get-tuple-element.130.high_ref, bf16[1024,64]{1,0:T(8,128)(2,1)S(1)} %broadcast_in_dim.40.pick_ref, f32[192,256]{1,0:T(8,128)S(1)} %copy-done.10, bf16[5,192,128]{2,1,0:T(8,128)(2,1)S(1)} %copy-done.1, ...), custom_call_target="tpu_custom_call" | custom-call | flops 10695475200 | bytes 7208960 | tf_op jit(solution)/shard_map/pallas_call | solution.py:246
  446.3 14.6 %shard_map.235 = (f32[5,192,128]{2,1,0:T(8,128)S(1)}, bf16[2048,640]{1,0:T(8,128)(2,1)}) custom-call(f32[1,2176]{1,0:T(1,128)S(1)} %get-tuple-element.131.high_ref, bf16[1024,64]{1,0:T(8,128)(2,1)S(1)} %broadcast_in_dim.46.pick_ref, f32[192,256]{1,0:T(8,128)S(1)} %copy-done.11, bf16[5,192,128]{2,1,0:T(8,128)(2,1)S(1)} %squeeze.106.q_ref, ...), custom_call_target="tpu_custom_call" | custom-call | flops 10695475200 | bytes 7208960 | tf_op jit(solution)/shard_map/pallas_call | solution.py:246
  465.6 14.5 %shard_map.234 = (f32[5,192,128]{2,1,0:T(8,128)S(1)}, bf16[2048,640]{1,0:T(8,128)(2,1)}) custom-call(f32[1,2176]{1,0:T(1,128)S(1)} %get-tuple-element.130.high_ref, bf16[1024,64]{1,0:T(8,128)(2,1)S(1)} %broadcast_in_dim.40.pick_ref, f32[192,256]{1,0:T(8,128)S(1)} %copy-done.11, bf16[5,192,128]{2,1,0:T(8,128)(2,1)S(1)} %squeeze.104.q_ref, ...), custom_call_target="tpu_custom_call" | custom-call | flops 10695475200 | bytes 7208960 | tf_op jit(solution)/shard_map/pallas_call | solution.py:246
  489.4 20.4 %rev.15 = f32[4,2,64,5,3,64]{2,1,5,4,3,0:T(2,128)} reverse(f32[4,2,64,5,3,64]{2,1,5,4,3,0:T(2,128)} %maximum_bitcast_fusion), dimensions={1} | reverse | bytes 3932160 | tf_op jit(solution)/shard_map/rev | solution.py:270
  547.0 10.9 %reshape.466 = bf16[2,2,640,960]{2,1,0,3:T(2,128)(2,1)} reshape(bf16[2560,960]{0,1:T(8,128)(2,1)} %bitcast_convert_fusion) | data formatting | bytes 9830400 | tf_op jit(solution)/shard_map/reshape | solution.py:89
  557.9 12.8 %constant_dynamic-slice_fusion.3 = (bf16[2,1,640,960]{2,1,0,3:T(2,128)(2,1)}, bf16[2,1,640,960]{2,1,0,3:T(2,128)(2,1)S(1)}) fusion(bf16[2,2,640,960]{2,1,0,3:T(2,128)(2,1)} %reshape.466, s32[]{:T(128)S(6)} %select_n.489, s32[]{:T(128)S(6)} %select_n.490), kind=kLoop, calls=%fused_computation.291 | loop fusion | bytes 9830408 | tf_op jit(solution)/shard_map/jit(dynamic_index_in_dim)/dynamic_slice | solution.py:90
  662.5 12.0 %collective-permute-start.82 = (bf16[2,640,960]{1,2,0:T(8,128)(2,1)}, bf16[2,640,960]{1,2,0:T(8,128)(2,1)}, u32[]{:S(2)}, u32[]{:S(2)}) collective-permute-start(bf16[2,640,960]{1,2,0:T(8,128)(2,1)} %bitcast.227), channel_id=1, source_target_pairs={{0,2},{2,0},{4,6},{6,4},{8,10},{10,8},{12,14},{14,12},{16,18},{18,... | collective-permute-start | bytes 7372808 | tf_op jit(solution)/shard_map/ppermute | solution.py:71
  720.8 10.4 %collective-permute-done.37 = bf16[128,640]{1,0:T(8,128)(2,1)S(1)} collective-permute-done((bf16[128,640]{1,0:T(8,128)(2,1)S(1)}, bf16[128,640]{1,0:T(8,128)(2,1)S(1)}, u32[]{:S(2)}, u32[]{:S(2)}) %collective-permute-start.37) | collective-permute-done | bytes 163872 | tf_op jit(solution)/shard_map/ppermute | solution.py:71
  731.2 8.7 collective-permute-done.33
  740.5 9.6 collective-permute-done.29
  780.3 76.8 %collective-permute-done.43 = bf16[240,704]{0,1:T(8,128)(2,1)S(1)} collective-permute-done((bf16[240,704]{0,1:T(8,128)(2,1)S(1)}, bf16[240,704]{0,1:T(8,128)(2,1)S(1)}, u32[]{:S(2)}, u32[]{:S(2)}) %collective-permute-start.43) | collective-permute-done | bytes 337952 | tf_op jit(solution)/shard_map/ppermute | solution.py:95
  867.5 8.8 collective-permute-done.46
  884.5 10.1 collective-permute-done.48
  916.0 11.5 %collective-permute-done.77 = bf16[240,640]{1,0:T(8,128)(2,1)} collective-permute-done((bf16[240,640]{1,0:T(8,128)(2,1)}, bf16[240,640]{1,0:T(8,128)(2,1)}, u32[]{:S(2)}, u32[]{:S(2)}) %collective-permute-start.77) | collective-permute-done | bytes 307232 | tf_op jit(solution)/shard_map/ppermute | solution.py:71
  928.6 10.0 collective-permute-done.85
  941.6 20.1 %collective-permute-done.78 = bf16[240,640]{1,0:T(8,128)(2,1)S(1)} collective-permute-done((bf16[240,640]{1,0:T(8,128)(2,1)S(1)}, bf16[240,640]{1,0:T(8,128)(2,1)S(1)}, u32[]{:S(2)}, u32[]{:S(2)}) %collective-permute-start.78) | collective-permute-done | bytes 307232 | tf_op jit(solution)/shard_map/ppermute | solution.py:71
  961.9 10.4 %collective-permute-done.86 = bf16[160,960]{0,1:T(8,128)(2,1)S(1)} collective-permute-done((bf16[160,960]{0,1:T(8,128)(2,1)S(1)}, bf16[160,960]{0,1:T(8,128)(2,1)S(1)}, u32[]{:S(2)}, u32[]{:S(2)}) %collective-permute-start.86) | collective-permute-done | bytes 307232 | tf_op jit(solution)/shard_map/ppermute | solution.py:71
  (693 shorter events, 615.2 us)
Async XLA Ops:
  13.6 51.3 %collective-permute-start.24 = (bf16[640,960]{0,1:T(8,128)(2,1)}, bf16[640,960]{0,1:T(8,128)(2,1)}, u32[]{:S(2)}, u32[]{:S(2)}) collective-permute-start(bf16[640,960]{0,1:T(8,128)(2,1)} %constant_dynamic-slice_fusion.14), channel_id=1, source_target_pairs={{0,1},{1,0},{2,3},{3,2},{4,5},{5,4},{6,7},{7,6},{8,9},{9,8},{10,11... | collective-permute-start | bytes 3686408 | tf_op jit(solution)/shard_map/ppermute | solution.py:60
  16.2 75.1 %collective-permute-start.20 = (bf16[240,2560]{1,0:T(8,128)(2,1)}, bf16[240,2560]{1,0:T(8,128)(2,1)}, u32[]{:S(2)}, u32[]{:S(2)}) collective-permute-start(bf16[240,2560]{1,0:T(8,128)(2,1)} %constant_dynamic-slice_fusion.16), channel_id=1, source_target_pairs={{0,1},{1,0},{2,3},{3,2},{4,5},{5,4},{6,7},{7,6},{8,9},{9,8},{10,11... | collective-permute-start | bytes 3686408 | tf_op jit(solution)/shard_map/ppermute | solution.py:60
  17.3 100.2 %collective-permute-start.22 = (bf16[240,2560]{1,0:T(8,128)(2,1)}, bf16[240,2560]{1,0:T(8,128)(2,1)}, u32[]{:S(2)}, u32[]{:S(2)}) collective-permute-start(bf16[240,2560]{1,0:T(8,128)(2,1)} %constant_dynamic-slice_fusion.15), channel_id=1, source_target_pairs={{0,1},{1,0},{2,3},{3,2},{4,5},{5,4},{6,7},{7,6},{8,9},{9,8},{10,11... | collective-permute-start | bytes 3686408 | tf_op jit(solution)/shard_map/ppermute | solution.py:60
  42.3 82.7 %collective-permute-start.1 = (bf16[240,1664]{1,0:T(8,128)(2,1)}, bf16[240,1664]{1,0:T(8,128)(2,1)S(1)}, u32[]{:S(2)}, u32[]{:S(2)}) collective-permute-start(bf16[240,1664]{1,0:T(8,128)(2,1)} %collective-permute-done), channel_id=1, source_target_pairs={{0,2},{2,0},{4,6},{6,4},{8,10},{10,8},{12,14},{14,12},{16,18},{18,... | collective-permute-start | bytes 2396168 | tf_op jit(solution)/shard_map/ppermute | solution.py:71
  64.9 144.9 %collective-permute-start.25 = (bf16[640,960]{0,1:T(8,128)(2,1)}, bf16[640,960]{0,1:T(8,128)(2,1)}, u32[]{:S(2)}, u32[]{:S(2)}) collective-permute-start(bf16[640,960]{0,1:T(8,128)(2,1)} %collective-permute-done.24), channel_id=1, source_target_pairs={{0,2},{2,0},{4,6},{6,4},{8,10},{10,8},{12,14},{14,12},{16,18},{18,... | collective-permute-start | bytes 3686408 | tf_op jit(solution)/shard_map/ppermute | solution.py:71
  91.2 129.8 %collective-permute-start.21 = (bf16[240,2560]{1,0:T(8,128)(2,1)}, bf16[240,2560]{1,0:T(8,128)(2,1)}, u32[]{:S(2)}, u32[]{:S(2)}) collective-permute-start(bf16[240,2560]{1,0:T(8,128)(2,1)} %collective-permute-done.20), channel_id=1, source_target_pairs={{0,2},{2,0},{4,6},{6,4},{8,10},{10,8},{12,14},{14,12},{16,18},{18,... | collective-permute-start | bytes 3686408 | tf_op jit(solution)/shard_map/ppermute | solution.py:71
  117.6 111.8 %collective-permute-start.23 = (bf16[240,2560]{1,0:T(8,128)(2,1)}, bf16[240,2560]{1,0:T(8,128)(2,1)}, u32[]{:S(2)}, u32[]{:S(2)}) collective-permute-start(bf16[240,2560]{1,0:T(8,128)(2,1)} %collective-permute-done.22), channel_id=1, source_target_pairs={{0,2},{2,0},{4,6},{6,4},{8,10},{10,8},{12,14},{14,12},{16,18},{18,... | collective-permute-start | bytes 3686408 | tf_op jit(solution)/shard_map/ppermute | solution.py:71
  135.6 39.7 %collective-permute-start.14 = (bf16[128,640]{1,0:T(8,128)(2,1)S(1)}, bf16[128,640]{1,0:T(8,128)(2,1)}, u32[]{:S(2)}, u32[]{:S(2)}) collective-permute-start(bf16[128,640]{1,0:T(8,128)(2,1)S(1)} %copy.162), channel_id=1, source_target_pairs={{0,16},{2,18},{4,20},{6,22},{8,24},{10,26},{12,28},{14,30},{16,0},... | collective-permute-start | bytes 491528 | tf_op jit(solution)/shard_map/ppermute | solution.py:71
  139.0 41.3 %collective-permute-start.10 = (bf16[128,640]{1,0:T(8,128)(2,1)S(1)}, bf16[128,640]{1,0:T(8,128)(2,1)}, u32[]{:S(2)}, u32[]{:S(2)}) collective-permute-start(bf16[128,640]{1,0:T(8,128)(2,1)S(1)} %copy.157), channel_id=1, source_target_pairs={{0,16},{2,18},{4,20},{6,22},{8,24},{10,26},{12,28},{14,30},{16,0},... | collective-permute-start | bytes 491528 | tf_op jit(solution)/shard_map/ppermute | solution.py:71
  240.7 37.6 %collective-permute-start.5 = (bf16[1024,640]{1,0:T(8,128)(2,1)}, bf16[1024,640]{1,0:T(8,128)(2,1)}, u32[]{:S(2)}, u32[]{:S(2)}) collective-permute-start(bf16[1024,640]{1,0:T(8,128)(2,1)} %pad_maximum_fusion.2), channel_id=1, source_target_pairs={{0,2},{2,0},{4,6},{6,4},{8,10},{10,8},{12,14},{14,12},{16,18},{18,... | collective-permute-start | bytes 3932168 | tf_op jit(solution)/shard_map/ppermute | solution.py:71
  536.5 49.1 %collective-permute-start.38 = (bf16[1024,640]{1,0:T(8,128)(2,1)}, bf16[1024,640]{1,0:T(8,128)(2,1)}, u32[]{:S(2)}, u32[]{:S(2)}) collective-permute-start(bf16[1024,640]{1,0:T(8,128)(2,1)} %slice.258), channel_id=1, source_target_pairs={{0,2},{2,0},{4,6},{6,4},{8,10},{10,8},{12,14},{14,12},{16,18},{18,... | collective-permute-start | bytes 3932168 | tf_op jit(solution)/shard_map/ppermute | solution.py:71
  538.7 49.3 %collective-permute-start.34 = (bf16[1024,640]{1,0:T(8,128)(2,1)}, bf16[1024,640]{1,0:T(8,128)(2,1)}, u32[]{:S(2)}, u32[]{:S(2)}) collective-permute-start(bf16[1024,640]{1,0:T(8,128)(2,1)} %slice.250), channel_id=1, source_target_pairs={{0,2},{2,0},{4,6},{6,4},{8,10},{10,8},{12,14},{14,12},{16,18},{18,... | collective-permute-start | bytes 3932168 | tf_op jit(solution)/shard_map/ppermute | solution.py:71
  540.4 50.8 %collective-permute-start.30 = (bf16[1024,640]{1,0:T(8,128)(2,1)}, bf16[1024,640]{1,0:T(8,128)(2,1)}, u32[]{:S(2)}, u32[]{:S(2)}) collective-permute-start(bf16[1024,640]{1,0:T(8,128)(2,1)} %slice.242), channel_id=1, source_target_pairs={{0,2},{2,0},{4,6},{6,4},{8,10},{10,8},{12,14},{14,12},{16,18},{18,... | collective-permute-start | bytes 3932168 | tf_op jit(solution)/shard_map/ppermute | solution.py:71
  583.7 178.6 %collective-permute-start.66 = (bf16[2,240,2560]{2,1,0:T(8,128)(2,1)}, bf16[2,240,2560]{2,1,0:T(8,128)(2,1)}, u32[]{:S(2)}, u32[]{:S(2)}) collective-permute-start(bf16[2,240,2560]{2,1,0:T(8,128)(2,1)} %dynamic-slice_bitcast_fusion.1), channel_id=1, source_target_pairs={{0,2},{2,0},{4,6},{6,4},{8,10},{10,8},{12,14},{14,12},{16,18},{18,... | collective-permute-start | bytes 7372808 | tf_op jit(solution)/shard_map/ppermute | solution.py:71
  585.6 183.0 %collective-permute-start.74 = (bf16[2,240,2560]{2,1,0:T(8,128)(2,1)}, bf16[2,240,2560]{2,1,0:T(8,128)(2,1)}, u32[]{:S(2)}, u32[]{:S(2)}) collective-permute-start(bf16[2,240,2560]{2,1,0:T(8,128)(2,1)} %dynamic-slice_bitcast_fusion), channel_id=1, source_target_pairs={{0,2},{2,0},{4,6},{6,4},{8,10},{10,8},{12,14},{14,12},{16,18},{18,... | collective-permute-start | bytes 7372808 | tf_op jit(solution)/shard_map/ppermute | solution.py:71
  593.2 67.3 %collective-permute-start.39 = (bf16[512,640]{1,0:T(8,128)(2,1)S(1)}, bf16[512,640]{1,0:T(8,128)(2,1)S(1)}, u32[]{:S(2)}, u32[]{:S(2)}) collective-permute-start(bf16[512,640]{1,0:T(8,128)(2,1)S(1)} %slice.318), channel_id=1, source_target_pairs={{0,8},{2,10},{4,12},{6,14},{8,0},{10,2},{12,4},{14,6},{16,24},{18,... | collective-permute-start | bytes 1966088 | tf_op jit(solution)/shard_map/ppermute | solution.py:71
  601.0 61.5 %collective-permute-start.35 = (bf16[512,640]{1,0:T(8,128)(2,1)S(1)}, bf16[512,640]{1,0:T(8,128)(2,1)S(1)}, u32[]{:S(2)}, u32[]{:S(2)}) collective-permute-start(bf16[512,640]{1,0:T(8,128)(2,1)S(1)} %slice.312), channel_id=1, source_target_pairs={{0,4},{2,6},{4,0},{6,2},{8,12},{10,14},{12,8},{14,10},{16,20},{18,... | collective-permute-start | bytes 1966088 | tf_op jit(solution)/shard_map/ppermute | solution.py:71
  662.5 110.6 %collective-permute-start.82 = (bf16[2,640,960]{1,2,0:T(8,128)(2,1)}, bf16[2,640,960]{1,2,0:T(8,128)(2,1)}, u32[]{:S(2)}, u32[]{:S(2)}) collective-permute-start(bf16[2,640,960]{1,2,0:T(8,128)(2,1)} %bitcast.227), channel_id=1, source_target_pairs={{0,2},{2,0},{4,6},{6,4},{8,10},{10,8},{12,14},{14,12},{16,18},{18,... | collective-permute-start | bytes 7372808 | tf_op jit(solution)/shard_map/ppermute | solution.py:71
  704.4 73.0 %collective-permute-start.57 = (bf16[240,960]{1,0:T(8,128)(2,1)}, bf16[240,960]{1,0:T(8,128)(2,1)}, u32[]{:S(2)}, u32[]{:S(2)}) collective-permute-start(bf16[240,960]{1,0:T(8,128)(2,1)} %pad_maximum_fusion.19), channel_id=1, source_target_pairs={{0,2},{2,0},{4,6},{6,4},{8,10},{10,8},{12,14},{14,12},{16,18},{18,... | collective-permute-start | bytes 1382408 | tf_op jit(solution)/shard_map/ppermute | solution.py:71
  768.7 93.9 %collective-permute-start.67 = (bf16[240,2560]{1,0:T(8,128)(2,1)S(1)}, bf16[240,2560]{1,0:T(8,128)(2,1)S(1)}, u32[]{:S(2)}, u32[]{:S(2)}) collective-permute-start(bf16[240,2560]{1,0:T(8,128)(2,1)S(1)} %dynamic-slice_bitcast_fusion.4), channel_id=1, source_target_pairs={{0,1},{1,0},{2,3},{3,2},{4,5},{5,4},{6,7},{7,6},{8,9},{9,8},{10,11... | collective-permute-start | bytes 3686408 | tf_op jit(solution)/shard_map/ppermute | solution.py:95
  773.1 94.1 %collective-permute-start.75 = (bf16[240,2560]{1,0:T(8,128)(2,1)S(1)}, bf16[240,2560]{1,0:T(8,128)(2,1)S(1)}, u32[]{:S(2)}, u32[]{:S(2)}) collective-permute-start(bf16[240,2560]{1,0:T(8,128)(2,1)S(1)} %dynamic-slice_bitcast_fusion.3), channel_id=1, source_target_pairs={{0,1},{1,0},{2,3},{3,2},{4,5},{5,4},{6,7},{7,6},{8,9},{9,8},{10,11... | collective-permute-start | bytes 3686408 | tf_op jit(solution)/shard_map/ppermute | solution.py:95
  775.9 106.3 %collective-permute-start.83 = (bf16[640,960]{0,1:T(8,128)(2,1)S(1)}, bf16[640,960]{0,1:T(8,128)(2,1)S(1)}, u32[]{:S(2)}, u32[]{:S(2)}) collective-permute-start(bf16[640,960]{0,1:T(8,128)(2,1)S(1)} %dynamic-slice_bitcast_fusion.2), channel_id=1, source_target_pairs={{0,1},{1,0},{2,3},{3,2},{4,5},{5,4},{6,7},{7,6},{8,9},{9,8},{10,11... | collective-permute-start | bytes 3686408 | tf_op jit(solution)/shard_map/ppermute | solution.py:95
  777.4 79.8 %collective-permute-start.43 = (bf16[240,704]{0,1:T(8,128)(2,1)S(1)}, bf16[240,704]{0,1:T(8,128)(2,1)S(1)}, u32[]{:S(2)}, u32[]{:S(2)}) collective-permute-start(bf16[240,704]{0,1:T(8,128)(2,1)S(1)} %dynamic-slice_bitcast_fusion.9), channel_id=1, source_target_pairs={{0,1},{1,0},{2,3},{3,2},{4,5},{5,4},{6,7},{7,6},{8,9},{9,8},{10,11... | collective-permute-start | bytes 1013768 | tf_op jit(solution)/shard_map/ppermute | solution.py:95
  863.7 38.9 %collective-permute-start.68 = (bf16[240,1280]{1,0:T(8,128)(2,1)}, bf16[240,1280]{1,0:T(8,128)(2,1)}, u32[]{:S(2)}, u32[]{:S(2)}) collective-permute-start(bf16[240,1280]{1,0:T(8,128)(2,1)} %constant_dynamic-slice_fusion.7), channel_id=1, source_target_pairs={{0,4},{2,6},{4,0},{6,2},{8,12},{10,14},{12,8},{14,10},{16,20},{18,... | collective-permute-start | bytes 1843208 | tf_op jit(solution)/shard_map/ppermute | solution.py:71
  (168 other events, 2164.5 us)

commit v2 on v1

v2 whole, which is shorter than its diff:
```python
import jax
import jax.numpy as jnp
from jax import lax
from jax.experimental import pallas as pl
from jax.experimental.pallas import tpu as pltpu
from jax.sharding import PartitionSpec as P

QH = 15
KVH = 5
HD = 64
GROUP = QH // KVH


EPS = 1e-05
THETA = 100000.0
FAR = -1e30


def place_rows(start_row, row_count, shard_rows, ctx_size):
    stored = start_row + jnp.arange(row_count, dtype=jnp.int32)
    half_rows = shard_rows // 2
    holder = stored // shard_rows
    within = stored % shard_rows
    mirror = (2 * ctx_size - 1 - holder) * half_rows + within - half_rows
    return jnp.where(within < half_rows, holder * half_rows + within, mirror)


def turn_tables(position, sign):
    frequency = THETA ** (-jnp.arange(0, HD, 2, dtype=jnp.float32) / HD)
    angles = position.astype(jnp.float32)[:, None] * frequency[None, :]
    cosine, sine = jnp.cos(angles), sign * jnp.sin(angles)
    cosine = jnp.concatenate([cosine, cosine], -1)
    sine = jnp.concatenate([-sine, sine], -1)
    still = jnp.ones_like(cosine)
    cosine = jnp.concatenate([cosine] * QH + [cosine, still] * KVH, -1)
    sine = jnp.concatenate([sine] * QH + [sine, 0.0 * still] * KVH, -1)
    return cosine, sine


def turn(flat, tables):
    cosine, sine = tables
    part = HD // 2
    after = jnp.concatenate([flat[..., part:], flat[..., :part]], -1)
    before = jnp.concatenate([flat[..., -part:], flat[..., :-part]], -1)
    first = jnp.arange(flat.shape[-1]) % HD < part
    return flat * cosine + jnp.where(first, after, before) * sine


def outer_sum(left, right):
    return lax.dot_general(
        left, right, (((0, 1), (0, 1)), ((), ())), preferred_element_type=jnp.float32
    )


def times_transposed(grad_in, weight):
    return lax.dot_general(
        grad_in, weight, (((2,), (1,)), ((), ())), preferred_element_type=jnp.float32
    )


def paired():
    size = lax.axis_size("ctx")
    return lax.axis_size("fsdp") == 2 and size >= 4 and not size & (size - 1)


def fetch_piece(shard):
    if not paired():
        return lax.all_gather(shard, "fsdp", axis=0, tiled=True)
    half = shard.shape[0] // 2
    core = lax.axis_index("ctx") & 1
    piece = lax.dynamic_slice_in_dim(shard, core * half, half, 0)
    return lax.ppermute(piece, "fsdp", [(0, 1), (1, 0)])


def fill_in(shard, got):
    if not paired():
        return got
    f = lax.axis_index("fsdp")
    core = lax.axis_index("ctx") & 1
    rows = shard.shape[0]
    half = rows // 2
    other = xor_permute(got, 1)
    full = jnp.zeros((2 * rows,) + shard.shape[1:], shard.dtype)
    full = lax.dynamic_update_slice_in_dim(full, shard, f * rows, 0)
    start = (1 - f) * rows
    full = lax.dynamic_update_slice_in_dim(full, got, start + core * half, 0)
    return lax.dynamic_update_slice_in_dim(full, other, start + (1 - core) * half, 0)


def xor_permute(array, mask):
    size = lax.axis_size("ctx")
    return lax.ppermute(array, "ctx", [(i, i ^ mask) for i in range(size)])


def add_low(kept, received):
    total = kept.astype(jnp.float32) + received.astype(jnp.float32)
    return total.astype(jnp.bfloat16)


def reduce_core(grad):
    grad = grad.astype(jnp.bfloat16)
    if not paired():
        return grad
    core = lax.axis_index("ctx") & 1
    rows, cols = grad.shape
    parts = grad.reshape(2, 2, rows // 4, cols)
    keep = lax.dynamic_index_in_dim(parts, core, 1, False)
    send = lax.dynamic_index_in_dim(parts, 1 - core, 1, False)
    return add_low(keep, xor_permute(send, 1))


def reduce_pair(total):
    if not paired():
        return lax.psum_scatter(total, "fsdp", scatter_dimension=0, tiled=True)
    f = lax.axis_index("fsdp")
    keep = lax.dynamic_index_in_dim(total, f, 0, False)
    send = lax.dynamic_index_in_dim(total, 1 - f, 0, False)
    return add_low(keep, lax.ppermute(send, "fsdp", [(0, 1), (1, 0)]))


def reduce_rest(total, split_dim):
    if not paired():
        return lax.psum(total, "ctx").astype(jnp.float32)
    size = lax.axis_size("ctx")
    c = lax.axis_index("ctx")
    masks = []
    mask = 2
    while mask < size:
        masks.append(mask)
        mask *= 2
    for mask in masks[:-1]:
        bit = (c // mask) % 2
        half = total.shape[split_dim] // 2
        keep = lax.dynamic_slice_in_dim(total, bit * half, half, split_dim)
        send = lax.dynamic_slice_in_dim(total, (1 - bit) * half, half, split_dim)
        total = add_low(keep, xor_permute(send, mask))
    total = add_low(total, xor_permute(total, masks[-1]))
    for mask in masks[:-1][::-1]:
        total = join(total, xor_permute(total, mask), (c // mask) % 2, split_dim)
    return join(total, xor_permute(total, 1), c & 1, 0).astype(jnp.float32)


def reduce_grad(grad, split_dim):
    return reduce_rest(reduce_pair(reduce_core(grad)), split_dim)


def after(arrays, *others):
    tied = lax.optimization_barrier((tuple(arrays), others))
    return tied[0]


def join(mine, theirs, bit, dim):
    first = jnp.where(bit == 0, mine, theirs)
    second = jnp.where(bit == 0, theirs, mine)
    return jnp.concatenate([first, second], dim)


def gather_order(size, which):
    masks = []
    mask = size // 2
    while mask:
        masks.append(mask)
        mask //= 2
    if which % 2 and len(masks) >= 4:
        masks[1:3] = masks[1:3][::-1]
    return masks


def holders(size, masks):
    offsets = [0]
    for mask in masks:
        offsets = offsets + [offset ^ mask for offset in offsets]
    return jnp.array(offsets, jnp.int32)


def block_parts(kv, pick):
    slots = kv.shape[0] // (4 * HD) * 2
    split = kv.reshape(slots, 2, HD, 2 * HD)
    low = split[:, 0].reshape(slots * HD, 2 * HD)
    high = split[:, 1].reshape(slots * HD, 2 * HD)
    nothing = jnp.zeros((slots * HD, HD), kv.dtype)
    nothing_own = jnp.zeros((2 * HD, HD), kv.dtype)
    rest = 1 - pick

    def of(at):
        lows, highs = low[:, at : at + HD], high[:, at : at + HD]
        return jnp.concatenate(
            [
                jnp.concatenate([nothing, lows], 1),
                jnp.concatenate([lows * rest, highs * pick], 1),
                jnp.concatenate([kv[: 2 * HD, at : at + HD], nothing_own], 1),
            ],
            0,
        )

    return of(0), of(HD)


def masked_scores(queries, keys, bias, wide):
    scores = lax.dot_general(
        queries, keys, (((1,), (1,)), ((), ())), preferred_element_type=jnp.float32
    )
    step = 2 * HD
    return jnp.concatenate(
        [
            scores[:, :wide],
            scores[:, wide : wide + step] + bias[:, :step],
            scores[:, wide + step : 2 * wide],
            scores[:, 2 * wide :] + bias[:, step:],
        ],
        1,
    )


def spread(low, high):
    shape = (high.shape[0], HD)
    return jnp.concatenate([jnp.broadcast_to(low, shape), jnp.broadcast_to(high, shape)], 1)


def stage_heads(flat_ref, staged_ref):
    for head in range(KVH):

        @pl.when(pl.program_id(0) == head)
        def _():
            for j in range(GROUP):
                at = (head * GROUP + j) * HD
                rows = slice(j * HD, (j + 1) * HD)
                staged_ref[rows, :HD] = flat_ref[0, :HD, at : at + HD]
                staged_ref[rows, HD:] = flat_ref[0, HD:, at : at + HD]


def unstage_heads(staged, flat_ref):
    for head in range(KVH):

        @pl.when(pl.program_id(0) == head)
        def _():
            for j in range(GROUP):
                at = (head * GROUP + j) * HD
                rows = slice(j * HD, (j + 1) * HD)
                flat_ref[:HD, at : at + HD] = staged[rows, :HD]
                flat_ref[HD:, at : at + HD] = staged[rows, HD:]


def forward_kernel(high_ref, pick_ref, bias_ref, q_ref, kv_ref, out_ref, norm_ref, flat_ref, q_rows):
    stage_heads(q_ref, q_rows)
    wide = pick_ref.shape[0]
    keys, values = block_parts(kv_ref[...], pick_ref[...])
    scores = masked_scores(q_rows[...], keys, bias_ref[...], wide)
    is_high = high_ref[...] > 0.5
    high_max = jnp.max(jnp.where(is_high, scores, FAR), 1, keepdims=True)
    low_max = jnp.max(jnp.where(is_high, FAR, scores), 1, keepdims=True)
    terms = jnp.exp(scores - jnp.where(is_high, high_max, low_max))
    high_sum = jnp.sum(jnp.where(is_high, terms, 0.0), 1, keepdims=True)
    low_sum = jnp.sum(jnp.where(is_high, 0.0, terms), 1, keepdims=True)
    mixed = jnp.dot(terms.astype(jnp.bfloat16), values, preferred_element_type=jnp.float32)
    mixed = mixed / spread(low_sum, high_sum)
    out_ref[0] = mixed
    unstage_heads(mixed.astype(jnp.bfloat16), flat_ref)
    norm_ref[0] = spread(low_max + jnp.log(low_sum), high_max + jnp.log(high_sum))


def backward_kernel(
    high_ref,
    pick_ref,
    bias_ref,
    q_ref,
    kv_ref,
    g_ref,
    out_ref,
    norm_ref,
    dq_ref,
    dkv_ref,
    q_rows,
    g_rows,
):
    stage_heads(q_ref, q_rows)
    stage_heads(g_ref, g_rows)
    wide = pick_ref.shape[0]
    pick = pick_ref[...]
    queries, grads = q_rows[...], g_rows[...]
    keys, values = block_parts(kv_ref[...], pick)
    scores = masked_scores(queries, keys, bias_ref[...], wide)
    is_high = high_ref[...] > 0.5
    norm = norm_ref[0]
    probs = jnp.exp(scores - jnp.where(is_high, norm[:, HD : HD + 1], norm[:, :1]))
    product = grads.astype(jnp.float32) * out_ref[0]
    high_delta = jnp.sum(product[:, HD:], 1, keepdims=True)
    low_delta = jnp.sum(product[:, :HD], 1, keepdims=True)
    dprobs = lax.dot_general(
        grads, values, (((1,), (1,)), ((), ())), preferred_element_type=jnp.float32
    )
    dscores = (probs * (dprobs - jnp.where(is_high, high_delta, low_delta))).astype(jnp.bfloat16)
    dquery = jnp.dot(dscores, keys, preferred_element_type=jnp.float32) * HD ** (-0.5)
    unstage_heads(dquery, dq_ref)
    over_rows = (((0,), (0,)), ((), ()))
    dkeys = lax.dot_general(dscores, queries, over_rows, preferred_element_type=jnp.float32)
    dvalues = lax.dot_general(
        probs.astype(jnp.bfloat16), grads, over_rows, preferred_element_type=jnp.float32
    )
    pick_wide = pick.astype(jnp.float32)

    def fold(terms):
        low = terms[:wide, HD:] + terms[wide : 2 * wide, :HD] * (1.0 - pick_wide)
        own = low[:HD] + terms[2 * wide : 2 * wide + HD, :HD]
        return jnp.concatenate([own, low[HD:]], 0), terms[wide : 2 * wide, HD:] * pick_wide

    low_k, high_k = fold(dkeys)
    low_v, high_v = fold(dvalues)
    slots = wide // HD
    low = jnp.concatenate([low_k, low_v], 1).astype(jnp.bfloat16).reshape(slots, 1, HD, 2 * HD)
    high = jnp.concatenate([high_k, high_v], 1).astype(jnp.bfloat16).reshape(slots, 1, HD, 2 * HD)
    dkv_ref[...] = jnp.concatenate([low, high], 1).reshape(dkv_ref.shape)


def attention_call(kernel, consts, flats, kept, kv, s, backward):
    high_row, pick, bias = consts
    wide = pick.shape[0]
    rows = GROUP * HD
    shard_rows, q_width = flats[0].shape[1:]
    whole = lambda array: pl.BlockSpec(array.shape, lambda g: (0, 0))
    flat = pl.BlockSpec((1, shard_rows, q_width), lambda g: (s, 0, 0))
    flat_out = pl.BlockSpec((shard_rows, q_width), lambda g: (0, 0))
    head = pl.BlockSpec((1, rows, 2 * HD), lambda g: (g, 0, 0))
    kv_spec = pl.BlockSpec((kv.shape[0], 2 * HD), lambda g: (0, g))
    head_shape = jax.ShapeDtypeStruct((KVH, rows, 2 * HD), jnp.float32)
    if backward:
        out_specs = [flat_out, kv_spec]
        out_shape = [
            jax.ShapeDtypeStruct((shard_rows, q_width), jnp.float32),
            jax.ShapeDtypeStruct(kv.shape, jnp.bfloat16),
        ]
    else:
        out_specs = [head, head, flat_out]
        out_shape = [
            head_shape,
            head_shape,
            jax.ShapeDtypeStruct((shard_rows, q_width), jnp.bfloat16),
        ]
    work = 2 * rows * (2 * wide + 2 * HD) * 2 * HD * KVH
    return pl.pallas_call(
        kernel,
        grid=(KVH,),
        in_specs=[whole(high_row), whole(pick), whole(bias), flat, kv_spec]
        + [flat] * (len(flats) - 1)
        + [head] * len(kept),
        out_specs=out_specs,
        out_shape=out_shape,
        scratch_shapes=[pltpu.VMEM((rows, 2 * HD), jnp.bfloat16)] * len(flats),
        compiler_params=pltpu.CompilerParams(vmem_limit_bytes=52 * 1024 * 1024),
        cost_estimate=pl.CostEstimate(
            flops=work * (80 if backward else 40),
            bytes_accessed=kv.size * (4 if backward else 2),
            transcendentals=rows * (2 * wide + 2 * HD) * KVH,
        ),
    )(high_row, pick, bias, flats[0], kv, *flats[1:], *kept)


def body(
    layer_input,
    out_grad,
    attn_gain,
    w_query,
    w_key,
    w_value,
    w_output,
    mlp_gain,
    w_gate,
    w_up,
    w_down,
):
    size = lax.axis_size("ctx")
    c = lax.axis_index("ctx")
    core = c & 1
    q_width, kv_width = QH * HD, KVH * HD
    gains = jnp.stack([attn_gain, mlp_gain], 1)
    gains = jnp.pad(gains, ((0, 0), (0, HD - 2)))
    pad_rows = w_key.shape[0]
    kv_weight = jnp.concatenate(
        [w_key.reshape(pad_rows, KVH, HD), w_value.reshape(pad_rows, KVH, HD)], -1
    ).reshape(pad_rows, 2 * kv_width)
    first = jnp.concatenate([w_query, kv_weight, gains], 1)
    first_got = fetch_piece(first)
    later = after((w_output, w_gate, w_up, w_down), first_got)
    later_got = [fetch_piece(weight) for weight in later]
    first_all = fill_in(first, first_got)
    proj_width = q_width + 2 * kv_width
    qkv_all = first_all[:, :proj_width]
    gain_first = first_all[:, proj_width].astype(jnp.float32)
    gain_mid = first_all[:, proj_width + 1].astype(jnp.float32)
    seq_count, shard_rows = (layer_input.shape[0], layer_input.shape[1])
    local_pos = place_rows(c * shard_rows, shard_rows, shard_rows, size)
    source = layer_input.astype(jnp.float32)
    inv_one = lax.rsqrt(jnp.mean(source * source, -1, keepdims=True) + EPS)
    normed_one = source * inv_one
    h_one = (normed_one * gain_first).astype(jnp.bfloat16)
    qkv = jnp.dot(h_one, qkv_all, preferred_element_type=jnp.float32)
    turned = turn(qkv, turn_tables(local_pos, 1.0)).astype(jnp.bfloat16)
    queries = turned[..., :q_width] * jnp.bfloat16(HD ** (-0.5))
    kv_local = turned[..., q_width:]

    within = jnp.arange(GROUP * HD, dtype=jnp.int32)[:, None] % HD
    tile = jnp.arange(4 * HD, dtype=jnp.int32)[None, :]
    first_tile = (tile < HD) & (tile > within)
    spare_tile = (tile >= 2 * HD) & (tile - 2 * HD > within)
    bias = jnp.where(first_tile | spare_tile, FAR, 0.0).astype(jnp.float32)
    gathered, orders, consts = [], [], []
    for s in range(seq_count):
        masks = gather_order(size, s)
        pieces = kv_local[s]
        for mask in masks:
            pieces = jnp.concatenate([pieces, xor_permute(pieces, mask)], 0)
        picks = jnp.repeat((holders(size, masks) ^ c) >= c, HD)
        high_row = jnp.concatenate(
            [jnp.ones(size * HD, bool), picks, jnp.zeros(2 * HD, bool)]
        ).astype(jnp.float32)[None, :]
        pick = jnp.broadcast_to(picks[:, None], (size * HD, HD)).astype(jnp.bfloat16)
        gathered.append(pieces)
        orders.append(masks)
        consts.append((high_row, pick, bias))
    kept, flats = [], []
    for s in range(seq_count):
        out, norm, flat = attention_call(
            forward_kernel, consts[s], (queries,), (), gathered[s], s, False
        )
        kept.append((out, norm))
        flats.append(flat)
    later_got = after(later_got, flats[min(1, seq_count - 1)])
    output_all, gate_all, up_all, down_all = [
        fill_in(shard, got) for shard, got in zip(later, later_got)
    ]
    attended = jnp.stack(flats)
    middle = source + jnp.dot(attended, output_all, preferred_element_type=jnp.float32)
    inv_two = lax.rsqrt(jnp.mean(middle * middle, -1, keepdims=True) + EPS)
    normed_two = middle * inv_two
    h_two = (normed_two * gain_mid).astype(jnp.bfloat16)
    gate = jnp.dot(h_two, gate_all, preferred_element_type=jnp.float32)
    up_proj = jnp.dot(h_two, up_all, preferred_element_type=jnp.float32)
    sigma = jax.nn.sigmoid(gate)
    silu_gate = gate * sigma
    hidden = (silu_gate * up_proj).astype(jnp.bfloat16)
    layer_output = (middle + jnp.dot(hidden, down_all, preferred_element_type=jnp.float32)).astype(
        jnp.bfloat16
    )
    g_hidden = times_transposed(out_grad, down_all)
    down_grad = outer_sum(hidden, out_grad)
    down_part = reduce_core(down_grad)
    gate_slope = sigma * (1.0 + gate * (1.0 - sigma))
    g_gate = (g_hidden * up_proj * gate_slope).astype(jnp.bfloat16)
    g_up = (g_hidden * silu_gate).astype(jnp.bfloat16)
    gate_grad = outer_sum(h_two, g_gate)
    up_grad = outer_sum(h_two, g_up)
    gate_part = reduce_core(gate_grad)
    up_part = reduce_core(up_grad)
    g_h_two = times_transposed(g_gate, gate_all) + times_transposed(g_up, up_all)
    mlp_gain_grad = jnp.sum(g_h_two * normed_two, (0, 1))
    g_normed_two = g_h_two * gain_mid
    g_middle = out_grad.astype(jnp.float32) + inv_two * (
        g_normed_two - normed_two * jnp.mean(g_normed_two * normed_two, -1, keepdims=True)
    )
    g_branch = g_middle.astype(jnp.bfloat16)
    output_grad = outer_sum(attended, g_branch)
    output_shard = reduce_grad(output_grad, 0)
    g_attended = times_transposed(g_branch, output_all).astype(jnp.bfloat16)
    (g_attended,) = after((g_attended,), down_part, gate_part, up_part)
    parts = [reduce_pair(part) for part in (down_part, gate_part, up_part)]
    dqueries, kv_grads = [], []
    for s in range(seq_count):
        grads = g_attended
        if s >= 2 and s - 2 < len(parts):
            (grads,) = after((grads,), parts[s - 2])
        dquery, term = attention_call(
            backward_kernel, consts[s], (queries, grads), kept[s], gathered[s], s, True
        )
        dqueries.append(dquery)
        for mask in orders[s][::-1]:
            half = term.shape[0] // 2
            term = add_low(term[:half], xor_permute(term[half:], mask))
        kv_grads.append(term)
    down_shard = reduce_rest(parts[0], 0)
    gate_shard = reduce_rest(parts[1], 1)
    up_shard = reduce_rest(parts[2], 1)
    cosine, sine = turn_tables(local_pos, -1.0)
    q_tables = (cosine[:, :q_width], sine[:, :q_width])
    kv_tables = (cosine[:, q_width:], sine[:, q_width:])
    g_query_proj = turn(jnp.stack(dqueries), q_tables).astype(jnp.bfloat16)
    query_shard = reduce_grad(outer_sum(h_one, g_query_proj), 0)
    g_kv = turn(jnp.stack(kv_grads).astype(jnp.float32), kv_tables).astype(jnp.bfloat16)
    g_h_one = times_transposed(
        jnp.concatenate([g_query_proj, g_kv], -1), qkv_all
    )
    attn_gain_grad = jnp.sum(g_h_one * normed_one, (0, 1))
    gain_grads = jnp.pad(jnp.stack([attn_gain_grad, mlp_gain_grad], 1), ((0, 0), (0, HD - 2)))
    last_shard = reduce_grad(jnp.concatenate([outer_sum(h_one, g_kv), gain_grads], 1), 0)
    kv_shard = last_shard[:, : 2 * kv_width].reshape(pad_rows, KVH, 2, HD)
    g_normed_one = g_h_one * gain_first
    input_grad = (
        g_middle
        + inv_one
        * (g_normed_one - normed_one * jnp.mean(g_normed_one * normed_one, -1, keepdims=True))
    ).astype(jnp.bfloat16)
    return (
        layer_output,
        input_grad,
        last_shard[:, 2 * kv_width],
        query_shard,
        kv_shard[:, :, 0].reshape(pad_rows, kv_width),
        kv_shard[:, :, 1].reshape(pad_rows, kv_width),
        output_shard,
        last_shard[:, 2 * kv_width + 1],
        gate_shard,
        up_shard,
        down_shard,
    )


def solution(mesh):
    in_specs = (
        P("fsdp", "ctx", None),
        P("fsdp", "ctx", None),
        P("fsdp"),
        P("fsdp", None),
        P("fsdp", None),
        P("fsdp", None),
        P("fsdp", None),
        P("fsdp"),
        P("fsdp", None),
        P("fsdp", None),
        P("fsdp", None),
    )
    out_specs = (
        P("fsdp", "ctx", None),
        P("fsdp", "ctx", None),
        P("fsdp"),
        P("fsdp", None),
        P("fsdp", None),
        P("fsdp", None),
        P("fsdp", None),
        P("fsdp"),
        P("fsdp", None),
        P("fsdp", None),
        P("fsdp", None),
    )
    return jax.shard_map(body, mesh=mesh, in_specs=in_specs, out_specs=out_specs, check_vma=False)
```

time: 1050 us -> 795 us (0.76)
  local copies, waits for them, and re-layouts: 292 us -> 120 us
  waiting for transfers between devices: 375 us -> 303 us
  Pallas kernels: 90.7 us -> 112 us
    rev x5 -> x0, local copies, waits for them, and re-layouts: 83.7 us -> none  [the longest x3 46.8 us: unstack_heads(): stacked.reshape(seqs, KVH, GROUP, HD, 2, HD).transpose(0, 4, 3, 1, 2, 5)]
    ppermute x11, waiting for transfers between devices: 164 us -> 81.5 us  [the longest x5 63.6 us: fetch_piece(): return lax.ppermute(piece, 'fsdp', [(0, 1), (1, 0)])]
    another operation x16 -> x4, local copies, waits for them, and re-layouts: 34.7 us -> 0.65 us  [the longest x8 18 us: body(): dquery_flat = unstack_heads(jnp.stack(dqueries))]
    reshape x6 -> x2, local copies, waits for them, and re-layouts: 35.7 us -> 11.2 us  [the longest x1 10.9 us: reduce_core(): parts = grad.reshape(2, 2, rows // 4, cols)]
    pallas_call x8, Pallas kernels: 90.7 us -> 112 us  [attention_call(): pl.pallas_call(kernel, grid=(KVH,), in_specs=[whole(high_row), whole(pick...]
    unnamed x220 -> x255, local copies, waits for them, and re-layouts: 38.2 us -> 17.3 us
    transpose x2 -> x0, other arithmetic: 11.5 us -> none  [unstack_heads(): stacked.reshape(seqs, KVH, GROUP, HD, 2, HD).transpose(0, 4, 3, 1, 2, 5)]
    ppermute x79, starting transfers between devices: 106 us -> 95.1 us  [xor_permute(): return lax.ppermute(array, 'ctx', [(i, i ^ mask) for i in range(size)])]
  transfers between devices with their start and end apart: 90 -> 90, of which waited for: 42 -> 41; matrix products, arithmetic and copies ran while one was open for 22% -> 28% of each run, Pallas kernels for 2% -> 14%
where the time goes in v2:
time: 795 us; the launch traced here: 789 us
  waiting for transfers between devices  303 us (38%)
  local copies, waits for them, and re-layouts  120 us (15%)
  Pallas kernels  112 us (14%)
  starting transfers between devices  107 us (13%)
  other arithmetic  87.6 us (11%)
  matrix products  56.9 us (7%)
    ppermute x79, waiting for transfers between devices, xor_permute(): return lax.ppermute(array, 'ctx', [(i, i ^ mask) for i in range(size)])  221 us
    pallas_call x8, Pallas kernels, attention_call(): pl.pallas_call(kernel, grid=(KVH,), in_specs=[whole(high_row), whole(pick...  112 us
    ppermute x79, starting transfers between devices, xor_permute(): return lax.ppermute(array, 'ctx', [(i, i ^ mask) for i in range(size)])  95.1 us
    ppermute x5, waiting for transfers between devices, fetch_piece(): return lax.ppermute(piece, 'fsdp', [(0, 1), (1, 0)])  63.6 us
    convert_element_type x42, other arithmetic, add_low(): return total.astype(jnp.bfloat16)  35.8 us
    dot_general x5, matrix products, times_transposed(): lax.dot_general(grad_in, weight, (((2,), (1,)), ((), ())), preferred_elem...  21 us
    ppermute x6, waiting for transfers between devices, reduce_pair(): return add_low(keep, lax.ppermute(send, 'fsdp', [(0, 1), (1, 0)]))  17.9 us
    unnamed x255, local copies, waits for them, and re-layouts  17.3 us
  transfers between devices with their start and end apart: 90, of which 41 were waited for; matrix products, arithmetic and copies ran while one was open for 28% of the time, Pallas kernels for 14%

profile of v2, /device:TPU:1, one launch (start us, length us, event | category | flops | bytes accessed | tf_op | source)
XLA Modules:
  0.0 789.4 jit_solution(2771459646254170001)
XLA Ops:
  52.7 15.6 %collective-permute-done.6 = bf16[128,640]{1,0:T(8,128)(2,1)S(1)} collective-permute-done((bf16[128,640]{1,0:T(8,128)(2,1)S(1)}, bf16[128,640]{1,0:T(8,128)(2,1)S(1)}, u32[]{:S(2)}, u32[]{:S(2)}) %collective-permute-start.6) | collective-permute-done | bytes 163872 | tf_op jit(solution)/shard_map/ppermute | solution.py:92
  93.9 12.8 %collective-permute-done.8 = bf16[512,640]{1,0:T(8,128)(2,1)S(1)} collective-permute-done((bf16[512,640]{1,0:T(8,128)(2,1)S(1)}, bf16[512,640]{1,0:T(8,128)(2,1)S(1)}, u32[]{:S(2)}, u32[]{:S(2)}) %collective-permute-start.8) | collective-permute-done | bytes 655392 | tf_op jit(solution)/shard_map/ppermute | solution.py:92
  108.6 12.1 %collective-permute-done.16 = bf16[512,640]{1,0:T(8,128)(2,1)S(1)} collective-permute-done((bf16[512,640]{1,0:T(8,128)(2,1)S(1)}, bf16[512,640]{1,0:T(8,128)(2,1)S(1)}, u32[]{:S(2)}, u32[]{:S(2)}) %collective-permute-start.16) | collective-permute-done | bytes 655392 | tf_op jit(solution)/shard_map/ppermute | solution.py:92
  130.5 9.6 %shard_map.231 = (f32[5,192,128]{2,1,0:T(8,128)S(1)}, f32[5,192,128]{2,1,0:T(8,128)S(1)}, bf16[128,960]{1,0:T(8,128)(2,1)S(1)}) custom-call(f32[1,2176]{1,0:T(1,128)S(1)} %get-tuple-element.156.high_ref, bf16[1024,64]{1,0:T(8,128)(2,1)S(1)} %broadcast_in_dim.102.pick_ref, f32[192,256]{1,0:T(8,128)S(1)} %fusion.78.bias_ref, ...), custom_call_target="tpu_custom_call" | custom-call | flops 21390950400 | bytes 2621440 | tf_op jit(solution)/shard_map/pallas_call | solution.py:340
  152.0 23.0 %collective-permute-done.20 = bf16[240,2560]{1,0:T(8,128)(2,1)} collective-permute-done((bf16[240,2560]{1,0:T(8,128)(2,1)}, bf16[240,2560]{1,0:T(8,128)(2,1)}, u32[]{:S(2)}, u32[]{:S(2)}) %collective-permute-start.20) | collective-permute-done | bytes 1228832 | tf_op jit(solution)/shard_map/ppermute | solution.py:72
  175.0 26.3 %collective-permute-done.21 = bf16[640,960]{0,1:T(8,128)(2,1)} collective-permute-done((bf16[640,960]{0,1:T(8,128)(2,1)}, bf16[640,960]{0,1:T(8,128)(2,1)}, u32[]{:S(2)}, u32[]{:S(2)}) %collective-permute-start.21) | collective-permute-done | bytes 1228832 | tf_op jit(solution)/shard_map/ppermute | solution.py:72
  204.3 9.6 %shard_map.233 = (f32[5,192,128]{2,1,0:T(8,128)S(1)}, f32[5,192,128]{2,1,0:T(8,128)S(1)}, bf16[128,960]{1,0:T(8,128)(2,1)S(1)}) custom-call(f32[1,2176]{1,0:T(1,128)S(1)} %get-tuple-element.156.high_ref, bf16[1024,64]{1,0:T(8,128)(2,1)S(1)} %broadcast_in_dim.102.pick_ref, f32[192,256]{1,0:T(8,128)S(1)} %fusion.78.bias_ref, ...), custom_call_target="tpu_custom_call" | custom-call | flops 21390950400 | bytes 2621440 | tf_op jit(solution)/shard_map/pallas_call | solution.py:340
  216.7 9.6 %shard_map.232 = (f32[5,192,128]{2,1,0:T(8,128)S(1)}, f32[5,192,128]{2,1,0:T(8,128)S(1)}, bf16[128,960]{1,0:T(8,128)(2,1)S(1)}) custom-call(f32[1,2176]{1,0:T(1,128)S(1)} %get-tuple-element.155.high_ref, bf16[1024,64]{1,0:T(8,128)(2,1)S(1)} %broadcast_in_dim.52.pick_ref, f32[192,256]{1,0:T(8,128)S(1)} %fusion.78.bias_ref, ...), custom_call_target="tpu_custom_call" | custom-call | flops 21390950400 | bytes 2621440 | tf_op jit(solution)/shard_map/pallas_call | solution.py:340
  228.7 10.0 %shard_map.230 = (f32[5,192,128]{2,1,0:T(8,128)S(1)}, f32[5,192,128]{2,1,0:T(8,128)S(1)}, bf16[128,960]{1,0:T(8,128)(2,1)S(1)}) custom-call(f32[1,2176]{1,0:T(1,128)S(1)} %get-tuple-element.155.high_ref, bf16[1024,64]{1,0:T(8,128)(2,1)S(1)} %broadcast_in_dim.52.pick_ref, f32[192,256]{1,0:T(8,128)S(1)} %fusion.78.bias_ref, ...), custom_call_target="tpu_custom_call" | custom-call | flops 21390950400 | bytes 2621440 | tf_op jit(solution)/shard_map/pallas_call | solution.py:340
  261.1 9.0 %fusion.1 = (bf16[4,128,2560]{2,1,0:T(8,128)(2,1)}, bf16[4,128,2560]{2,1,0:T(8,128)(2,1)}, bf16[4,128,2560]{2,1,0:T(8,128)(2,1)}) fusion(f32[2560,4,128]{0,2,1:T(8,128)} %fusion.7, f32[4,128,2560]{2,1,0:T(8,128)S(1)} %fusion.17, bf16[4,128,960]{1,2,0:T(8,128)(2,1)S(1)} %multiply_convert_fusion.1, bf16[960,2560]{1,0:T(8,128)(2,1)S(1)} %constant_dynamic-update-slice_fusion.23), kind=kOutput, calls=%fused_computation.6 | convolution fusion | flops 2536243200 | bytes 24248320 | tf_op jit(solution)/shard_map/dot_general | solution.py:437
  287.0 10.9 %reshape.337 = bf16[2,2,640,960]{2,1,0,3:T(2,128)(2,1)} reshape(bf16[2560,960]{0,1:T(8,128)(2,1)} %bitcast_convert_fusion.2) | data formatting | bytes 9830400 | tf_op jit(solution)/shard_map/reshape | solution.py:106
  297.9 11.9 %constant_dynamic-slice_fusion.13 = (bf16[2,1,640,960]{2,1,0,3:T(2,128)(2,1)S(1)}, bf16[2,1,640,960]{2,1,0,3:T(2,128)(2,1)S(1)}) fusion(bf16[2,2,640,960]{2,1,0,3:T(2,128)(2,1)} %reshape.337, s32[]{:T(128)S(6)} %select_n.514, s32[]{:T(128)S(6)} %select_n.515), kind=kLoop, calls=%fused_computation.284 | loop fusion | bytes 9830408 | tf_op jit(solution)/shard_map/jit(dynamic_index_in_dim)/dynamic_slice | solution.py:107
  368.0 18.3 %shard_map.235 = (f32[128,960]{1,0:T(8,128)S(1)}, bf16[2048,640]{1,0:T(8,128)(2,1)}) custom-call(f32[1,2176]{1,0:T(1,128)S(1)} %get-tuple-element.156.high_ref, bf16[1024,64]{1,0:T(8,128)(2,1)S(1)} %broadcast_in_dim.102.pick_ref, f32[192,256]{1,0:T(8,128)S(1)} %fusion.78.bias_ref, bf16[4,128,960]{2,1,0:T(8,128)(2,1)} %slice_multiply_fusion.q_ref, ...), custom_call_target="tpu_custom_call" | custom-call | flops 42781900800 | bytes 5242880 | tf_op jit(solution)/shard_map/pallas_call | solution.py:340
  389.5 18.7 %shard_map.234 = (f32[128,960]{1,0:T(8,128)S(1)}, bf16[2048,640]{1,0:T(8,128)(2,1)}) custom-call(f32[1,2176]{1,0:T(1,128)S(1)} %get-tuple-element.155.high_ref, bf16[1024,64]{1,0:T(8,128)(2,1)S(1)} %broadcast_in_dim.52.pick_ref, f32[192,256]{1,0:T(8,128)S(1)} %fusion.78.bias_ref, bf16[4,128,960]{2,1,0:T(8,128)(2,1)} %slice_multiply_fusion.q_ref, ...), custom_call_target="tpu_custom_call" | custom-call | flops 42781900800 | bytes 5242880 | tf_op jit(solution)/shard_map/pallas_call | solution.py:340
  424.5 18.3 %shard_map.237 = (f32[128,960]{1,0:T(8,128)S(1)}, bf16[2048,640]{1,0:T(8,128)(2,1)}) custom-call(f32[1,2176]{1,0:T(1,128)S(1)} %get-tuple-element.156.high_ref, bf16[1024,64]{1,0:T(8,128)(2,1)S(1)} %broadcast_in_dim.102.pick_ref, f32[192,256]{1,0:T(8,128)S(1)} %fusion.78.bias_ref, bf16[4,128,960]{2,1,0:T(8,128)(2,1)} %slice_multiply_fusion.q_ref, ...), custom_call_target="tpu_custom_call" | custom-call | flops 42781900800 | bytes 5242880 | tf_op jit(solution)/shard_map/pallas_call | solution.py:340
  442.7 18.4 %shard_map.236 = (f32[128,960]{1,0:T(8,128)S(1)}, bf16[2048,640]{1,0:T(8,128)(2,1)}) custom-call(f32[1,2176]{1,0:T(1,128)S(1)} %get-tuple-element.155.high_ref, bf16[1024,64]{1,0:T(8,128)(2,1)S(1)} %broadcast_in_dim.52.pick_ref, f32[192,256]{1,0:T(8,128)S(1)} %fusion.78.bias_ref, bf16[4,128,960]{2,1,0:T(8,128)(2,1)} %slice_multiply_fusion.q_ref, ...), custom_call_target="tpu_custom_call" | custom-call | flops 42781900800 | bytes 5242880 | tf_op jit(solution)/shard_map/pallas_call | solution.py:340
  485.5 8.6 %collective-permute-done.71 = bf16[240,1280]{1,0:T(8,128)(2,1)S(1)} collective-permute-done((bf16[240,1280]{1,0:T(8,128)(2,1)S(1)}, bf16[240,1280]{1,0:T(8,128)(2,1)S(1)}, u32[]{:S(2)}, u32[]{:S(2)}) %collective-permute-start.71) | collective-permute-done | bytes 614432 | tf_op jit(solution)/shard_map/ppermute | solution.py:92
  496.2 11.0 %collective-permute-done.78 = bf16[240,1280]{1,0:T(8,128)(2,1)S(1)} collective-permute-done((bf16[240,1280]{1,0:T(8,128)(2,1)S(1)}, bf16[240,1280]{1,0:T(8,128)(2,1)S(1)}, u32[]{:S(2)}, u32[]{:S(2)}) %collective-permute-start.78) | collective-permute-done | bytes 614432 | tf_op jit(solution)/shard_map/ppermute | solution.py:92
  509.4 12.0 %collective-permute-done.84 = bf16[320,960]{1,0:T(8,128)(2,1)S(1)} collective-permute-done((bf16[320,960]{1,0:T(8,128)(2,1)S(1)}, bf16[320,960]{1,0:T(8,128)(2,1)S(1)}, u32[]{:S(2)}, u32[]{:S(2)}) %collective-permute-start.84) | collective-permute-done | bytes 614432 | tf_op jit(solution)/shard_map/ppermute | solution.py:92
  569.5 22.4 %collective-permute-done.38 = bf16[128,640]{1,0:T(8,128)(2,1)S(1)} collective-permute-done((bf16[128,640]{1,0:T(8,128)(2,1)S(1)}, bf16[128,640]{1,0:T(8,128)(2,1)S(1)}, u32[]{:S(2)}, u32[]{:S(2)}) %collective-permute-start.38) | collective-permute-done | bytes 163872 | tf_op jit(solution)/shard_map/ppermute | solution.py:92
  591.9 7.8 collective-permute-done.34
  604.4 18.7 %collective-permute-done.86 = bf16[160,960]{0,1:T(8,128)(2,1)S(1)} collective-permute-done((bf16[160,960]{0,1:T(8,128)(2,1)S(1)}, bf16[160,960]{0,1:T(8,128)(2,1)S(1)}, u32[]{:S(2)}, u32[]{:S(2)}) %collective-permute-start.86) | collective-permute-done | bytes 307232 | tf_op jit(solution)/shard_map/ppermute | solution.py:92
  634.2 15.4 %collective-permute-done.57 = bf16[120,960]{1,0:T(8,128)(2,1)S(1)} collective-permute-done((bf16[120,960]{1,0:T(8,128)(2,1)S(1)}, bf16[120,960]{1,0:T(8,128)(2,1)S(1)}, u32[]{:S(2)}, u32[]{:S(2)}) %collective-permute-start.57) | collective-permute-done | bytes 230432 | tf_op jit(solution)/shard_map/ppermute | solution.py:92
  709.4 9.3 %collective-permute-done.46 = bf16[128,640]{1,0:T(8,128)(2,1)S(1)} collective-permute-done((bf16[128,640]{1,0:T(8,128)(2,1)S(1)}, bf16[128,640]{1,0:T(8,128)(2,1)S(1)}, u32[]{:S(2)}, u32[]{:S(2)}) %collective-permute-start.46) | collective-permute-done | bytes 163872 | tf_op jit(solution)/shard_map/ppermute | solution.py:92
  (678 shorter events, 446.7 us)
Async XLA Ops:
  25.6 115.3 %collective-permute-start.18 = (bf16[240,960]{1,0:T(8,128)(2,1)}, bf16[240,960]{1,0:T(8,128)(2,1)}, u32[]{:S(2)}, u32[]{:S(2)}) collective-permute-start(bf16[240,960]{1,0:T(8,128)(2,1)} %constant_dynamic-slice_fusion.17), channel_id=1, source_target_pairs={{0,1},{1,0},{2,3},{3,2},{4,5},{5,4},{6,7},{7,6},{8,9},{9,8},{10,11... | collective-permute-start | bytes 1382408 | tf_op jit(solution)/shard_map/ppermute | solution.py:72
  83.6 37.1 %collective-permute-start.16 = (bf16[512,640]{1,0:T(8,128)(2,1)S(1)}, bf16[512,640]{1,0:T(8,128)(2,1)S(1)}, u32[]{:S(2)}, u32[]{:S(2)}) collective-permute-start(bf16[512,640]{1,0:T(8,128)(2,1)S(1)} %pad_maximum_fusion.14), channel_id=1, source_target_pairs={{0,8},{2,10},{4,12},{6,14},{8,0},{10,2},{12,4},{14,6},{16,24},{18,... | collective-permute-start | bytes 1966088 | tf_op jit(solution)/shard_map/ppermute | solution.py:92
  121.9 53.1 %collective-permute-start.20 = (bf16[240,2560]{1,0:T(8,128)(2,1)}, bf16[240,2560]{1,0:T(8,128)(2,1)}, u32[]{:S(2)}, u32[]{:S(2)}) collective-permute-start(bf16[240,2560]{1,0:T(8,128)(2,1)} %constant_dynamic-slice_fusion.15), channel_id=1, source_target_pairs={{0,1},{1,0},{2,3},{3,2},{4,5},{5,4},{6,7},{7,6},{8,9},{9,8},{10,11... | collective-permute-start | bytes 3686408 | tf_op jit(solution)/shard_map/ppermute | solution.py:72
  122.5 78.8 %collective-permute-start.21 = (bf16[640,960]{0,1:T(8,128)(2,1)}, bf16[640,960]{0,1:T(8,128)(2,1)}, u32[]{:S(2)}, u32[]{:S(2)}) collective-permute-start(bf16[640,960]{0,1:T(8,128)(2,1)} %constant_dynamic-slice_fusion.14), channel_id=1, source_target_pairs={{0,1},{1,0},{2,3},{3,2},{4,5},{5,4},{6,7},{7,6},{8,9},{9,8},{10,11... | collective-permute-start | bytes 3686408 | tf_op jit(solution)/shard_map/ppermute | solution.py:72
  126.6 76.6 %collective-permute-start.17 = (bf16[1024,640]{1,0:T(8,128)(2,1)S(1)}, bf16[1024,640]{1,0:T(8,128)(2,1)S(1)}, u32[]{:S(2)}, u32[]{:S(2)}) collective-permute-start(bf16[1024,640]{1,0:T(8,128)(2,1)S(1)} %pad_maximum_fusion.4), channel_id=1, source_target_pairs={{0,2},{2,0},{4,6},{6,4},{8,10},{10,8},{12,14},{14,12},{16,18},{18,... | collective-permute-start | bytes 3932168 | tf_op jit(solution)/shard_map/ppermute | solution.py:92
  140.9 73.0 %collective-permute-start.13 = (bf16[1024,640]{1,0:T(8,128)(2,1)S(1)}, bf16[1024,640]{1,0:T(8,128)(2,1)}, u32[]{:S(2)}, u32[]{:S(2)}) collective-permute-start(bf16[1024,640]{1,0:T(8,128)(2,1)S(1)} %pad_maximum_fusion.3), channel_id=1, source_target_pairs={{0,2},{2,0},{4,6},{6,4},{8,10},{10,8},{12,14},{14,12},{16,18},{18,... | collective-permute-start | bytes 3932168 | tf_op jit(solution)/shard_map/ppermute | solution.py:92
  148.6 77.6 %collective-permute-start.5 = (bf16[1024,640]{1,0:T(8,128)(2,1)}, bf16[1024,640]{1,0:T(8,128)(2,1)}, u32[]{:S(2)}, u32[]{:S(2)}) collective-permute-start(bf16[1024,640]{1,0:T(8,128)(2,1)} %pad_maximum_fusion.1), channel_id=1, source_target_pairs={{0,2},{2,0},{4,6},{6,4},{8,10},{10,8},{12,14},{14,12},{16,18},{18,... | collective-permute-start | bytes 3932168 | tf_op jit(solution)/shard_map/ppermute | solution.py:92
  201.3 45.9 %collective-permute-start.22 = (bf16[240,960]{1,0:T(8,128)(2,1)}, bf16[240,960]{1,0:T(8,128)(2,1)S(1)}, u32[]{:S(2)}, u32[]{:S(2)}) collective-permute-start(bf16[240,960]{1,0:T(8,128)(2,1)} %collective-permute-done.18), channel_id=1, source_target_pairs={{0,2},{2,0},{4,6},{6,4},{8,10},{10,8},{12,14},{14,12},{16,18},{18,... | collective-permute-start | bytes 1382408 | tf_op jit(solution)/shard_map/ppermute | solution.py:92
  354.7 56.0 %collective-permute-start.70 = (bf16[240,960]{1,0:T(8,128)(2,1)}, bf16[240,960]{1,0:T(8,128)(2,1)}, u32[]{:S(2)}, u32[]{:S(2)}) collective-permute-start(bf16[240,960]{1,0:T(8,128)(2,1)} %pad_maximum_fusion.18), channel_id=1, source_target_pairs={{0,2},{2,0},{4,6},{6,4},{8,10},{10,8},{12,14},{14,12},{16,18},{18,... | collective-permute-start | bytes 1382408 | tf_op jit(solution)/shard_map/ppermute | solution.py:92
  366.6 48.0 %collective-permute-start.30 = (bf16[240,2560]{1,0:T(8,128)(2,1)}, bf16[240,2560]{1,0:T(8,128)(2,1)}, u32[]{:S(2)}, u32[]{:S(2)}) collective-permute-start(bf16[240,2560]{1,0:T(8,128)(2,1)} %dynamic-slice_bitcast_fusion.3), channel_id=1, source_target_pairs={{0,1},{1,0},{2,3},{3,2},{4,5},{5,4},{6,7},{7,6},{8,9},{9,8},{10,11... | collective-permute-start | bytes 3686408 | tf_op jit(solution)/shard_map/ppermute | solution.py:118
  367.6 54.3 %collective-permute-start.29 = (bf16[640,960]{0,1:T(8,128)(2,1)S(1)}, bf16[640,960]{0,1:T(8,128)(2,1)}, u32[]{:S(2)}, u32[]{:S(2)}) collective-permute-start(bf16[640,960]{0,1:T(8,128)(2,1)S(1)} %dynamic-slice_bitcast_fusion.4), channel_id=1, source_target_pairs={{0,1},{1,0},{2,3},{3,2},{4,5},{5,4},{6,7},{7,6},{8,9},{9,8},{10,11... | collective-permute-start | bytes 3686408 | tf_op jit(solution)/shard_map/ppermute | solution.py:118
  388.9 89.6 %collective-permute-start.35 = (bf16[1024,640]{1,0:T(8,128)(2,1)}, bf16[1024,640]{1,0:T(8,128)(2,1)}, u32[]{:S(2)}, u32[]{:S(2)}) collective-permute-start(bf16[1024,640]{1,0:T(8,128)(2,1)} %slice.209), channel_id=1, source_target_pairs={{0,2},{2,0},{4,6},{6,4},{8,10},{10,8},{12,14},{14,12},{16,18},{18,... | collective-permute-start | bytes 3932168 | tf_op jit(solution)/shard_map/ppermute | solution.py:92
  410.7 70.7 %collective-permute-start.31 = (bf16[1024,640]{1,0:T(8,128)(2,1)}, bf16[1024,640]{1,0:T(8,128)(2,1)}, u32[]{:S(2)}, u32[]{:S(2)}) collective-permute-start(bf16[1024,640]{1,0:T(8,128)(2,1)} %slice.201), channel_id=1, source_target_pairs={{0,2},{2,0},{4,6},{6,4},{8,10},{10,8},{12,14},{14,12},{16,18},{18,... | collective-permute-start | bytes 3932168 | tf_op jit(solution)/shard_map/ppermute | solution.py:92
  410.7 65.4 %collective-permute-start.77 = (bf16[240,2560]{1,0:T(8,128)(2,1)}, bf16[240,2560]{1,0:T(8,128)(2,1)}, u32[]{:S(2)}, u32[]{:S(2)}) collective-permute-start(bf16[240,2560]{1,0:T(8,128)(2,1)} %dynamic-slice_bitcast_fusion.2), channel_id=1, source_target_pairs={{0,1},{1,0},{2,3},{3,2},{4,5},{5,4},{6,7},{7,6},{8,9},{9,8},{10,11... | collective-permute-start | bytes 3686408 | tf_op jit(solution)/shard_map/ppermute | solution.py:118
  464.4 158.8 %collective-permute-start.43 = (bf16[1024,640]{1,0:T(8,128)(2,1)}, bf16[1024,640]{1,0:T(8,128)(2,1)}, u32[]{:S(2)}, u32[]{:S(2)}) collective-permute-start(bf16[1024,640]{1,0:T(8,128)(2,1)} %slice.225), channel_id=1, source_target_pairs={{0,2},{2,0},{4,6},{6,4},{8,10},{10,8},{12,14},{14,12},{16,18},{18,... | collective-permute-start | bytes 3932168 | tf_op jit(solution)/shard_map/ppermute | solution.py:92
  466.7 160.6 %collective-permute-start.39 = (bf16[1024,640]{1,0:T(8,128)(2,1)}, bf16[1024,640]{1,0:T(8,128)(2,1)}, u32[]{:S(2)}, u32[]{:S(2)}) collective-permute-start(bf16[1024,640]{1,0:T(8,128)(2,1)} %slice.217), channel_id=1, source_target_pairs={{0,2},{2,0},{4,6},{6,4},{8,10},{10,8},{12,14},{14,12},{16,18},{18,... | collective-permute-start | bytes 3932168 | tf_op jit(solution)/shard_map/ppermute | solution.py:92
  476.1 65.8 %collective-permute-start.55 = (bf16[2,240,960]{2,1,0:T(8,128)(2,1)}, bf16[2,240,960]{2,1,0:T(8,128)(2,1)}, u32[]{:S(2)}, u32[]{:S(2)}) collective-permute-start(bf16[2,240,960]{2,1,0:T(8,128)(2,1)} %dynamic-slice_bitcast_fusion.6), channel_id=1, source_target_pairs={{0,2},{2,0},{4,6},{6,4},{8,10},{10,8},{12,14},{14,12},{16,18},{18,... | collective-permute-start | bytes 2764808 | tf_op jit(solution)/shard_map/ppermute | solution.py:92
  554.0 76.1 %collective-permute-start.56 = (bf16[240,960]{1,0:T(8,128)(2,1)S(1)}, bf16[240,960]{1,0:T(8,128)(2,1)S(1)}, u32[]{:S(2)}, u32[]{:S(2)}) collective-permute-start(bf16[240,960]{1,0:T(8,128)(2,1)S(1)} %dynamic-slice_bitcast_fusion.8), channel_id=1, source_target_pairs={{0,1},{1,0},{2,3},{3,2},{4,5},{5,4},{6,7},{7,6},{8,9},{9,8},{10,11... | collective-permute-start | bytes 1382408 | tf_op jit(solution)/shard_map/ppermute | solution.py:118
  627.3 45.8 %collective-permute-start.44 = (bf16[512,640]{1,0:T(8,128)(2,1)}, bf16[512,640]{1,0:T(8,128)(2,1)}, u32[]{:S(2)}, u32[]{:S(2)}) collective-permute-start(bf16[512,640]{1,0:T(8,128)(2,1)} %slice.276), channel_id=1, source_target_pairs={{0,8},{2,10},{4,12},{6,14},{8,0},{10,2},{12,4},{14,6},{16,24},{18,... | collective-permute-start | bytes 1966088 | tf_op jit(solution)/shard_map/ppermute | solution.py:92
  630.1 45.5 %collective-permute-start.40 = (bf16[512,640]{1,0:T(8,128)(2,1)}, bf16[512,640]{1,0:T(8,128)(2,1)}, u32[]{:S(2)}, u32[]{:S(2)}) collective-permute-start(bf16[512,640]{1,0:T(8,128)(2,1)} %slice.270), channel_id=1, source_target_pairs={{0,4},{2,6},{4,0},{6,2},{8,12},{10,14},{12,8},{14,10},{16,20},{18,... | collective-permute-start | bytes 1966088 | tf_op jit(solution)/shard_map/ppermute | solution.py:92
  633.0 45.1 %collective-permute-start.75 = (bf16[240,1280]{1,0:T(8,128)(2,1)}, bf16[240,1280]{1,0:T(8,128)(2,1)}, u32[]{:S(2)}, u32[]{:S(2)}) collective-permute-start(bf16[240,1280]{1,0:T(8,128)(2,1)} %pad_maximum_fusion.15), channel_id=1, source_target_pairs={{0,4},{2,6},{4,0},{6,2},{8,12},{10,14},{12,8},{14,10},{16,20},{18,... | collective-permute-start | bytes 1843208 | tf_op jit(solution)/shard_map/ppermute | solution.py:92
  681.5 69.7 %collective-permute-start.76 = (bf16[240,2560]{1,0:T(8,128)(2,1)}, bf16[240,2560]{1,0:T(8,128)(2,1)}, u32[]{:S(2)}, u32[]{:S(2)}) collective-permute-start(bf16[240,2560]{1,0:T(8,128)(2,1)} %pad_maximum_fusion.5), channel_id=1, source_target_pairs={{0,2},{2,0},{4,6},{6,4},{8,10},{10,8},{12,14},{14,12},{16,18},{18,... | collective-permute-start | bytes 3686408 | tf_op jit(solution)/shard_map/ppermute | solution.py:92
  691.0 65.3 %collective-permute-start.83 = (bf16[240,2560]{1,0:T(8,128)(2,1)}, bf16[240,2560]{1,0:T(8,128)(2,1)}, u32[]{:S(2)}, u32[]{:S(2)}) collective-permute-start(bf16[240,2560]{1,0:T(8,128)(2,1)} %pad_maximum_fusion.6), channel_id=1, source_target_pairs={{0,2},{2,0},{4,6},{6,4},{8,10},{10,8},{12,14},{14,12},{16,18},{18,... | collective-permute-start | bytes 3686408 | tf_op jit(solution)/shard_map/ppermute | solution.py:92
  702.9 72.0 %collective-permute-start.89 = (bf16[640,960]{0,1:T(8,128)(2,1)}, bf16[640,960]{0,1:T(8,128)(2,1)}, u32[]{:S(2)}, u32[]{:S(2)}) collective-permute-start(bf16[640,960]{0,1:T(8,128)(2,1)} %pad_maximum_fusion.7), channel_id=1, source_target_pairs={{0,2},{2,0},{4,6},{6,4},{8,10},{10,8},{12,14},{14,12},{16,18},{18,... | collective-permute-start | bytes 3686408 | tf_op jit(solution)/shard_map/ppermute | solution.py:92
  (187 other events, 1835.1 us)

commit v3 on v2

--- a/solution.py
+++ b/solution.py
@@ -118,7 +118,7 @@
     return add_low(keep, lax.ppermute(send, "fsdp", [(0, 1), (1, 0)]))
 
 
-def reduce_rest(total, split_dim):
+def reduce_rest(total, split_dim, swapped=False):
     if not paired():
         return lax.psum(total, "ctx").astype(jnp.float32)
     size = lax.axis_size("ctx")
@@ -128,6 +128,8 @@
     while mask < size:
         masks.append(mask)
         mask *= 2
+    if swapped and len(masks) > 2:
+        masks[:2] = masks[:2][::-1]
     for mask in masks[:-1]:
         bit = (c // mask) % 2
         half = total.shape[split_dim] // 2
@@ -407,7 +409,9 @@
     for s in range(seq_count):
         masks = gather_order(size, s)
         pieces = kv_local[s]
-        for mask in masks:
+        for step, mask in enumerate(masks):
+            if step == 2 and s < 3:
+                (pieces,) = after((pieces,), later_got[(0, 3, 1)[s]])
             pieces = jnp.concatenate([pieces, xor_permute(pieces, mask)], 0)
         picks = jnp.repeat((holders(size, masks) ^ c) >= c, HD)
         high_row = jnp.concatenate(
@@ -419,8 +423,9 @@
         consts.append((high_row, pick, bias))
     kept, flats = [], []
     for s in range(seq_count):
+        fed = queries if s != 1 else after((queries,), later_got[2])[0]
         out, norm, flat = attention_call(
-            forward_kernel, consts[s], (queries,), (), gathered[s], s, False
+            forward_kernel, consts[s], (fed,), (), gathered[s], s, False
         )
         kept.append((out, norm))
         flats.append(flat)
@@ -476,8 +481,9 @@
             half = term.shape[0] // 2
             term = add_low(term[:half], xor_permute(term[half:], mask))
         kv_grads.append(term)
+    parts = after(parts, *kv_grads[-2:])
     down_shard = reduce_rest(parts[0], 0)
-    gate_shard = reduce_rest(parts[1], 1)
+    gate_shard = reduce_rest(parts[1], 1, True)
     up_shard = reduce_rest(parts[2], 1)
     cosine, sine = turn_tables(local_pos, -1.0)
     q_tables = (cosine[:, :q_width], sine[:, :q_width])

time: 795 us -> 706 us (0.89)
  waiting for transfers between devices: 303 us -> 244 us
  local copies, waits for them, and re-layouts: 120 us -> 107 us
  other arithmetic: 87.6 us -> 76.7 us
    ppermute x79, waiting for transfers between devices: 221 us -> 191 us  [xor_permute(): return lax.ppermute(array, 'ctx', [(i, i ^ mask) for i in range(size)])]
    ppermute x5, waiting for transfers between devices: 63.6 us -> 44.4 us  [fetch_piece(): return lax.ppermute(piece, 'fsdp', [(0, 1), (1, 0)])]
    ppermute x6, waiting for transfers between devices: 17.9 us -> 8.65 us  [reduce_pair(): return add_low(keep, lax.ppermute(send, 'fsdp', [(0, 1), (1, 0)]))]
    convert_element_type x42 -> x44, other arithmetic: 35.8 us -> 27.1 us  [add_low(): return total.astype(jnp.bfloat16)]
    unnamed x255 -> x182, local copies, waits for them, and re-layouts: 17.3 us -> 13 us
  transfers between devices with their start and end apart: 90 -> 90, of which waited for: 41 -> 37; matrix products, arithmetic and copies ran while one was open for 28% -> 28% of each run, Pallas kernels for 14% -> 16%
where the time goes in v3:
time: 706 us; the launch traced here: 701 us
  waiting for transfers between devices  244 us (35%)
  Pallas kernels  112 us (16%)
  local copies, waits for them, and re-layouts  107 us (15%)
  starting transfers between devices  103 us (15%)
  other arithmetic  76.7 us (11%)
  matrix products  54.5 us (8%)
    ppermute x79, waiting for transfers between devices, xor_permute(): return lax.ppermute(array, 'ctx', [(i, i ^ mask) for i in range(size)])  191 us
    pallas_call x8, Pallas kernels, attention_call(): pl.pallas_call(kernel, grid=(KVH,), in_specs=[whole(high_row), whole(pick...  112 us
    ppermute x79, starting transfers between devices, xor_permute(): return lax.ppermute(array, 'ctx', [(i, i ^ mask) for i in range(size)])  93.4 us
    ppermute x5, waiting for transfers between devices, fetch_piece(): return lax.ppermute(piece, 'fsdp', [(0, 1), (1, 0)])  44.4 us
    convert_element_type x44, other arithmetic, add_low(): return total.astype(jnp.bfloat16)  27.1 us
    dot_general x5, matrix products, times_transposed(): lax.dot_general(grad_in, weight, (((2,), (1,)), ((), ())), preferred_elem...  18.4 us
    dot_general x6, matrix products, outer_sum(): lax.dot_general(left, right, (((0, 1), (0, 1)), ((), ())), preferred_elem...  15.1 us
  transfers between devices with their start and end apart: 90, of which 37 were waited for; matrix products, arithmetic and copies ran while one was open for 28% of the time, Pallas kernels for 16%

profile of v3, /device:TPU:1, one launch (start us, length us, event | category | flops | bytes accessed | tf_op | source)
XLA Modules:
  0.0 701.3 jit_solution(8249262714865166240)
XLA Ops:
  48.0 9.6 %collective-permute-done.8 = bf16[128,640]{1,0:T(8,128)(2,1)S(1)} collective-permute-done((bf16[128,640]{1,0:T(8,128)(2,1)S(1)}, bf16[128,640]{1,0:T(8,128)(2,1)S(1)}, u32[]{:S(2)}, u32[]{:S(2)}) %collective-permute-start.8) | collective-permute-done | bytes 163872 | tf_op jit(solution)/shard_map/ppermute | solution.py:92
  69.5 37.9 %collective-permute-done.10 = bf16[640,960]{0,1:T(8,128)(2,1)} collective-permute-done((bf16[640,960]{0,1:T(8,128)(2,1)}, bf16[640,960]{0,1:T(8,128)(2,1)}, u32[]{:S(2)}, u32[]{:S(2)}) %collective-permute-start.10) | collective-permute-done | bytes 1228832 | tf_op jit(solution)/shard_map/ppermute | solution.py:72
  116.5 19.1 %collective-permute-done.3 = bf16[256,640]{1,0:T(8,128)(2,1)S(1)} collective-permute-done((bf16[256,640]{1,0:T(8,128)(2,1)S(1)}, bf16[256,640]{1,0:T(8,128)(2,1)S(1)}, u32[]{:S(2)}, u32[]{:S(2)}) %collective-permute-start.3) | collective-permute-done | bytes 327712 | tf_op jit(solution)/shard_map/ppermute | solution.py:92
  160.1 9.6 %shard_map.231 = (f32[5,192,128]{2,1,0:T(8,128)S(1)}, f32[5,192,128]{2,1,0:T(8,128)S(1)}, bf16[128,960]{1,0:T(8,128)(2,1)S(1)}) custom-call(f32[1,2176]{1,0:T(1,128)S(1)} %get-tuple-element.166.high_ref, bf16[1024,64]{1,0:T(8,128)(2,1)S(1)} %broadcast_in_dim.102.pick_ref, f32[192,256]{1,0:T(8,128)S(1)} %fusion.78.bias_ref, ...), custom_call_target="tpu_custom_call" | custom-call | flops 21390950400 | bytes 2621440 | tf_op jit(solution)/shard_map/pallas_call | solution.py:342
  172.4 9.6 %shard_map.233 = (f32[5,192,128]{2,1,0:T(8,128)S(1)}, f32[5,192,128]{2,1,0:T(8,128)S(1)}, bf16[128,960]{1,0:T(8,128)(2,1)S(1)}) custom-call(f32[1,2176]{1,0:T(1,128)S(1)} %get-tuple-element.166.high_ref, bf16[1024,64]{1,0:T(8,128)(2,1)S(1)} %broadcast_in_dim.102.pick_ref, f32[192,256]{1,0:T(8,128)S(1)} %fusion.78.bias_ref, ...), custom_call_target="tpu_custom_call" | custom-call | flops 21390950400 | bytes 2621440 | tf_op jit(solution)/shard_map/pallas_call | solution.py:342
  184.7 9.6 %shard_map.232 = (f32[5,192,128]{2,1,0:T(8,128)S(1)}, f32[5,192,128]{2,1,0:T(8,128)S(1)}, bf16[128,960]{1,0:T(8,128)(2,1)S(1)}) custom-call(f32[1,2176]{1,0:T(1,128)S(1)} %get-tuple-element.165.high_ref, bf16[1024,64]{1,0:T(8,128)(2,1)S(1)} %broadcast_in_dim.52.pick_ref, f32[192,256]{1,0:T(8,128)S(1)} %fusion.78.bias_ref, ...), custom_call_target="tpu_custom_call" | custom-call | flops 21390950400 | bytes 2621440 | tf_op jit(solution)/shard_map/pallas_call | solution.py:342
  195.5 10.0 %shard_map.230 = (f32[5,192,128]{2,1,0:T(8,128)S(1)}, f32[5,192,128]{2,1,0:T(8,128)S(1)}, bf16[128,960]{1,0:T(8,128)(2,1)S(1)}) custom-call(f32[1,2176]{1,0:T(1,128)S(1)} %get-tuple-element.165.high_ref, bf16[1024,64]{1,0:T(8,128)(2,1)S(1)} %broadcast_in_dim.52.pick_ref, f32[192,256]{1,0:T(8,128)S(1)} %fusion.78.bias_ref, ...), custom_call_target="tpu_custom_call" | custom-call | flops 21390950400 | bytes 2621440 | tf_op jit(solution)/shard_map/pallas_call | solution.py:342
  226.2 9.1 %fusion.1 = (bf16[4,128,2560]{2,1,0:T(8,128)(2,1)}, bf16[4,128,2560]{2,1,0:T(8,128)(2,1)}, bf16[4,128,2560]{2,1,0:T(8,128)(2,1)}) fusion(f32[2560,4,128]{0,2,1:T(8,128)} %fusion.7, f32[4,128,2560]{2,1,0:T(8,128)S(1)} %fusion.17, bf16[4,128,960]{1,2,0:T(8,128)(2,1)S(1)} %multiply_convert_fusion.1, bf16[960,2560]{1,0:T(8,128)(2,1)S(1)} %constant_dynamic-update-slice_fusion.17), kind=kOutput, calls=%fused_computation.6 | convolution fusion | flops 2536243200 | bytes 24248320 | tf_op jit(solution)/shard_map/dot_general | solution.py:442
  251.6 10.9 %reshape.337 = bf16[2,2,640,960]{2,1,0,3:T(2,128)(2,1)} reshape(bf16[2560,960]{0,1:T(8,128)(2,1)} %bitcast_convert_fusion.2) | data formatting | bytes 9830400 | tf_op jit(solution)/shard_map/reshape | solution.py:106
  262.6 11.9 %constant_dynamic-slice_fusion.13 = (bf16[2,1,640,960]{2,1,0,3:T(2,128)(2,1)S(1)}, bf16[2,1,640,960]{2,1,0,3:T(2,128)(2,1)S(1)}) fusion(bf16[2,2,640,960]{2,1,0,3:T(2,128)(2,1)} %reshape.337, s32[]{:T(128)S(6)} %select_n.526, s32[]{:T(128)S(6)} %select_n.527), kind=kLoop, calls=%fused_computation.276 | loop fusion | bytes 9830408 | tf_op jit(solution)/shard_map/jit(dynamic_index_in_dim)/dynamic_slice | solution.py:107
  330.6 18.2 %shard_map.235 = (f32[128,960]{1,0:T(8,128)S(1)}, bf16[2048,640]{1,0:T(8,128)(2,1)}) custom-call(f32[1,2176]{1,0:T(1,128)S(1)} %get-tuple-element.166.high_ref, bf16[1024,64]{1,0:T(8,128)(2,1)S(1)} %broadcast_in_dim.102.pick_ref, f32[192,256]{1,0:T(8,128)S(1)} %fusion.78.bias_ref, bf16[4,128,960]{2,1,0:T(8,128)(2,1)} %slice_multiply_fusion.q_ref, ...), custom_call_target="tpu_custom_call" | custom-call | flops 42781900800 | bytes 5242880 | tf_op jit(solution)/shard_map/pallas_call | solution.py:342
  352.1 18.7 %shard_map.234 = (f32[128,960]{1,0:T(8,128)S(1)}, bf16[2048,640]{1,0:T(8,128)(2,1)}) custom-call(f32[1,2176]{1,0:T(1,128)S(1)} %get-tuple-element.165.high_ref, bf16[1024,64]{1,0:T(8,128)(2,1)S(1)} %broadcast_in_dim.52.pick_ref, f32[192,256]{1,0:T(8,128)S(1)} %fusion.78.bias_ref, bf16[4,128,960]{2,1,0:T(8,128)(2,1)} %slice_multiply_fusion.q_ref, ...), custom_call_target="tpu_custom_call" | custom-call | flops 42781900800 | bytes 5242880 | tf_op jit(solution)/shard_map/pallas_call | solution.py:342
  381.5 18.3 %shard_map.237 = (f32[128,960]{1,0:T(8,128)S(1)}, bf16[2048,640]{1,0:T(8,128)(2,1)}) custom-call(f32[1,2176]{1,0:T(1,128)S(1)} %get-tuple-element.166.high_ref, bf16[1024,64]{1,0:T(8,128)(2,1)S(1)} %broadcast_in_dim.102.pick_ref, f32[192,256]{1,0:T(8,128)S(1)} %fusion.78.bias_ref, bf16[4,128,960]{2,1,0:T(8,128)(2,1)} %slice_multiply_fusion.q_ref, ...), custom_call_target="tpu_custom_call" | custom-call | flops 42781900800 | bytes 5242880 | tf_op jit(solution)/shard_map/pallas_call | solution.py:342
  404.7 18.4 %shard_map.236 = (f32[128,960]{1,0:T(8,128)S(1)}, bf16[2048,640]{1,0:T(8,128)(2,1)}) custom-call(f32[1,2176]{1,0:T(1,128)S(1)} %get-tuple-element.165.high_ref, bf16[1024,64]{1,0:T(8,128)(2,1)S(1)} %broadcast_in_dim.52.pick_ref, f32[192,256]{1,0:T(8,128)S(1)} %fusion.78.bias_ref, bf16[4,128,960]{2,1,0:T(8,128)(2,1)} %slice_multiply_fusion.q_ref, ...), custom_call_target="tpu_custom_call" | custom-call | flops 42781900800 | bytes 5242880 | tf_op jit(solution)/shard_map/pallas_call | solution.py:342
  437.1 10.0 %collective-permute-done.36 = bf16[512,640]{1,0:T(8,128)(2,1)S(1)} collective-permute-done((bf16[512,640]{1,0:T(8,128)(2,1)S(1)}, bf16[512,640]{1,0:T(8,128)(2,1)S(1)}, u32[]{:S(2)}, u32[]{:S(2)}) %collective-permute-start.36) | collective-permute-done | bytes 655392 | tf_op jit(solution)/shard_map/ppermute | solution.py:92
  462.8 7.9 %collective-permute-done.38 = bf16[128,640]{1,0:T(8,128)(2,1)S(1)} collective-permute-done((bf16[128,640]{1,0:T(8,128)(2,1)S(1)}, bf16[128,640]{1,0:T(8,128)(2,1)S(1)}, u32[]{:S(2)}, u32[]{:S(2)}) %collective-permute-start.38) | collective-permute-done | bytes 163872 | tf_op jit(solution)/shard_map/ppermute | solution.py:92
  478.6 11.1 %collective-permute-done.59 = bf16[60,960]{1,0:T(8,128)(2,1)S(1)} collective-permute-done((bf16[60,960]{1,0:T(8,128)(2,1)S(1)}, bf16[60,960]{1,0:T(8,128)(2,1)S(1)}, u32[]{:S(2)}, u32[]{:S(2)}) %collective-permute-start.59) | collective-permute-done | bytes 115232 | tf_op jit(solution)/shard_map/ppermute | solution.py:92
  501.9 6.8 collective-permute-start.62
  511.4 10.1 %collective-permute-done.46 = bf16[128,640]{1,0:T(8,128)(2,1)S(1)} collective-permute-done((bf16[128,640]{1,0:T(8,128)(2,1)S(1)}, bf16[128,640]{1,0:T(8,128)(2,1)S(1)}, u32[]{:S(2)}, u32[]{:S(2)}) %collective-permute-start.46) | collective-permute-done | bytes 163872 | tf_op jit(solution)/shard_map/ppermute | solution.py:92
  563.7 9.3 %collective-permute-done.84 = bf16[320,960]{1,0:T(8,128)(2,1)} collective-permute-done((bf16[320,960]{1,0:T(8,128)(2,1)}, bf16[320,960]{1,0:T(8,128)(2,1)}, u32[]{:S(2)}, u32[]{:S(2)}) %collective-permute-start.84) | collective-permute-done | bytes 614432 | tf_op jit(solution)/shard_map/ppermute | solution.py:92
  596.3 16.3 %collective-permute-done.50 = bf16[60,704]{0,1:T(8,128)(2,1)S(1)} collective-permute-done((bf16[60,704]{0,1:T(8,128)(2,1)S(1)}, bf16[60,704]{0,1:T(8,128)(2,1)S(1)}, u32[]{:S(2)}, u32[]{:S(2)}) %collective-permute-start.50) | collective-permute-done | bytes 84512 | tf_op jit(solution)/shard_map/ppermute | solution.py:92
  621.8 16.2 %collective-permute-done.51 = bf16[60,704]{0,1:T(8,128)(2,1)S(1)} collective-permute-done((bf16[60,704]{0,1:T(8,128)(2,1)S(1)}, bf16[60,704]{0,1:T(8,128)(2,1)S(1)}, u32[]{:S(2)}, u32[]{:S(2)}) %collective-permute-start.51) | collective-permute-done | bytes 84512 | tf_op jit(solution)/shard_map/ppermute | solution.py:92
  639.8 9.9 %collective-permute-done.52 = bf16[60,704]{0,1:T(8,128)(2,1)S(1)} collective-permute-done((bf16[60,704]{0,1:T(8,128)(2,1)S(1)}, bf16[60,704]{0,1:T(8,128)(2,1)S(1)}, u32[]{:S(2)}, u32[]{:S(2)}) %collective-permute-start.52) | collective-permute-done | bytes 84512 | tf_op jit(solution)/shard_map/ppermute | solution.py:92
  666.7 6.9 collective-permute-done.76
  (606 shorter events, 382.9 us)
Async XLA Ops:
  27.2 88.0 %collective-permute-start.15 = (bf16[240,2560]{1,0:T(8,128)(2,1)}, bf16[240,2560]{1,0:T(8,128)(2,1)}, u32[]{:S(2)}, u32[]{:S(2)}) collective-permute-start(bf16[240,2560]{1,0:T(8,128)(2,1)} %constant_dynamic-slice_fusion.14), channel_id=1, source_target_pairs={{0,1},{1,0},{2,3},{3,2},{4,5},{5,4},{6,7},{7,6},{8,9},{9,8},{10,11... | collective-permute-start | bytes 3686408 | tf_op jit(solution)/shard_map/ppermute | solution.py:72
  29.5 79.5 %collective-permute-start.7 = (bf16[240,2560]{1,0:T(8,128)(2,1)}, bf16[240,2560]{1,0:T(8,128)(2,1)}, u32[]{:S(2)}, u32[]{:S(2)}) collective-permute-start(bf16[240,2560]{1,0:T(8,128)(2,1)} %constant_dynamic-slice_fusion.16), channel_id=1, source_target_pairs={{0,1},{1,0},{2,3},{3,2},{4,5},{5,4},{6,7},{7,6},{8,9},{9,8},{10,11... | collective-permute-start | bytes 3686408 | tf_op jit(solution)/shard_map/ppermute | solution.py:72
  30.9 76.5 %collective-permute-start.10 = (bf16[640,960]{0,1:T(8,128)(2,1)}, bf16[640,960]{0,1:T(8,128)(2,1)}, u32[]{:S(2)}, u32[]{:S(2)}) collective-permute-start(bf16[640,960]{0,1:T(8,128)(2,1)} %constant_dynamic-slice_fusion.15), channel_id=1, source_target_pairs={{0,1},{1,0},{2,3},{3,2},{4,5},{5,4},{6,7},{7,6},{8,9},{9,8},{10,11... | collective-permute-start | bytes 3686408 | tf_op jit(solution)/shard_map/ppermute | solution.py:72
  68.2 40.2 %collective-permute-start.2 = (bf16[128,640]{1,0:T(8,128)(2,1)S(1)}, bf16[128,640]{1,0:T(8,128)(2,1)S(1)}, u32[]{:S(2)}, u32[]{:S(2)}) collective-permute-start(bf16[128,640]{1,0:T(8,128)(2,1)S(1)} %get-tuple-element.123), channel_id=1, source_target_pairs={{0,16},{2,18},{4,20},{6,22},{8,24},{10,26},{12,28},{14,30},{16,0},... | collective-permute-start | bytes 491528 | tf_op jit(solution)/shard_map/ppermute | solution.py:92
  68.2 41.7 %collective-permute-start.19 = (bf16[256,640]{1,0:T(8,128)(2,1)S(1)}, bf16[256,640]{1,0:T(8,128)(2,1)S(1)}, u32[]{:S(2)}, u32[]{:S(2)}) collective-permute-start(bf16[256,640]{1,0:T(8,128)(2,1)S(1)} %pad_maximum_fusion.23), channel_id=1, source_target_pairs={{0,4},{2,6},{4,0},{6,2},{8,12},{10,14},{12,8},{14,10},{16,20},{18,... | collective-permute-start | bytes 983048 | tf_op jit(solution)/shard_map/ppermute | solution.py:92
  114.5 35.1 %collective-permute-start.20 = (bf16[512,640]{1,0:T(8,128)(2,1)S(1)}, bf16[512,640]{1,0:T(8,128)(2,1)S(1)}, u32[]{:S(2)}, u32[]{:S(2)}) collective-permute-start(bf16[512,640]{1,0:T(8,128)(2,1)S(1)} %pad_maximum_fusion.14), channel_id=1, source_target_pairs={{0,8},{2,10},{4,12},{6,14},{8,0},{10,2},{12,4},{14,6},{16,24},{18,... | collective-permute-start | bytes 1966088 | tf_op jit(solution)/shard_map/ppermute | solution.py:92
  115.2 37.7 %collective-permute-start.16 = (bf16[512,640]{1,0:T(8,128)(2,1)S(1)}, bf16[512,640]{1,0:T(8,128)(2,1)S(1)}, u32[]{:S(2)}, u32[]{:S(2)}) collective-permute-start(bf16[512,640]{1,0:T(8,128)(2,1)S(1)} %pad_maximum_fusion.13), channel_id=1, source_target_pairs={{0,4},{2,6},{4,0},{6,2},{8,12},{10,14},{12,8},{14,10},{16,20},{18,... | collective-permute-start | bytes 1966088 | tf_op jit(solution)/shard_map/ppermute | solution.py:92
  155.2 39.1 %collective-permute-start.6 = (bf16[1024,640]{1,0:T(8,128)(2,1)}, bf16[1024,640]{1,0:T(8,128)(2,1)S(1)}, u32[]{:S(2)}, u32[]{:S(2)}) collective-permute-start(bf16[1024,640]{1,0:T(8,128)(2,1)} %pad_maximum_fusion.1), channel_id=1, source_target_pairs={{0,2},{2,0},{4,6},{6,4},{8,10},{10,8},{12,14},{14,12},{16,18},{18,... | collective-permute-start | bytes 3932168 | tf_op jit(solution)/shard_map/ppermute | solution.py:92
  169.7 44.6 %collective-permute-start.22 = (bf16[240,960]{1,0:T(8,128)(2,1)}, bf16[240,960]{1,0:T(8,128)(2,1)}, u32[]{:S(2)}, u32[]{:S(2)}) collective-permute-start(bf16[240,960]{1,0:T(8,128)(2,1)} %collective-permute-done.4), channel_id=1, source_target_pairs={{0,2},{2,0},{4,6},{6,4},{8,10},{10,8},{12,14},{14,12},{16,18},{18,... | collective-permute-start | bytes 1382408 | tf_op jit(solution)/shard_map/ppermute | solution.py:92
  317.3 57.1 %collective-permute-start.70 = (bf16[240,960]{1,0:T(8,128)(2,1)}, bf16[240,960]{1,0:T(8,128)(2,1)}, u32[]{:S(2)}, u32[]{:S(2)}) collective-permute-start(bf16[240,960]{1,0:T(8,128)(2,1)} %pad_maximum_fusion.18), channel_id=1, source_target_pairs={{0,2},{2,0},{4,6},{6,4},{8,10},{10,8},{12,14},{14,12},{16,18},{18,... | collective-permute-start | bytes 1382408 | tf_op jit(solution)/shard_map/ppermute | solution.py:92
  329.1 49.0 %collective-permute-start.30 = (bf16[240,2560]{1,0:T(8,128)(2,1)}, bf16[240,2560]{1,0:T(8,128)(2,1)}, u32[]{:S(2)}, u32[]{:S(2)}) collective-permute-start(bf16[240,2560]{1,0:T(8,128)(2,1)} %dynamic-slice_bitcast_fusion.3), channel_id=1, source_target_pairs={{0,1},{1,0},{2,3},{3,2},{4,5},{5,4},{6,7},{7,6},{8,9},{9,8},{10,11... | collective-permute-start | bytes 3686408 | tf_op jit(solution)/shard_map/ppermute | solution.py:118
  330.0 73.1 %collective-permute-start.29 = (bf16[640,960]{0,1:T(8,128)(2,1)}, bf16[640,960]{0,1:T(8,128)(2,1)}, u32[]{:S(2)}, u32[]{:S(2)}) collective-permute-start(bf16[640,960]{0,1:T(8,128)(2,1)} %dynamic-slice_bitcast_fusion.4), channel_id=1, source_target_pairs={{0,1},{1,0},{2,3},{3,2},{4,5},{5,4},{6,7},{7,6},{8,9},{9,8},{10,11... | collective-permute-start | bytes 3686408 | tf_op jit(solution)/shard_map/ppermute | solution.py:118
  351.5 77.1 %collective-permute-start.35 = (bf16[1024,640]{1,0:T(8,128)(2,1)}, bf16[1024,640]{1,0:T(8,128)(2,1)}, u32[]{:S(2)}, u32[]{:S(2)}) collective-permute-start(bf16[1024,640]{1,0:T(8,128)(2,1)} %slice.209), channel_id=1, source_target_pairs={{0,2},{2,0},{4,6},{6,4},{8,10},{10,8},{12,14},{14,12},{16,18},{18,... | collective-permute-start | bytes 3932168 | tf_op jit(solution)/shard_map/ppermute | solution.py:92
  373.3 57.8 %collective-permute-start.31 = (bf16[1024,640]{1,0:T(8,128)(2,1)}, bf16[1024,640]{1,0:T(8,128)(2,1)}, u32[]{:S(2)}, u32[]{:S(2)}) collective-permute-start(bf16[1024,640]{1,0:T(8,128)(2,1)} %slice.201), channel_id=1, source_target_pairs={{0,2},{2,0},{4,6},{6,4},{8,10},{10,8},{12,14},{14,12},{16,18},{18,... | collective-permute-start | bytes 3932168 | tf_op jit(solution)/shard_map/ppermute | solution.py:92
  374.4 58.7 %collective-permute-start.71 = (bf16[240,2560]{1,0:T(8,128)(2,1)}, bf16[240,2560]{1,0:T(8,128)(2,1)}, u32[]{:S(2)}, u32[]{:S(2)}) collective-permute-start(bf16[240,2560]{1,0:T(8,128)(2,1)} %dynamic-slice_bitcast_fusion.2), channel_id=1, source_target_pairs={{0,1},{1,0},{2,3},{3,2},{4,5},{5,4},{6,7},{7,6},{8,9},{9,8},{10,11... | collective-permute-start | bytes 3686408 | tf_op jit(solution)/shard_map/ppermute | solution.py:118
  402.3 68.7 %collective-permute-start.43 = (bf16[1024,640]{1,0:T(8,128)(2,1)}, bf16[1024,640]{1,0:T(8,128)(2,1)}, u32[]{:S(2)}, u32[]{:S(2)}) collective-permute-start(bf16[1024,640]{1,0:T(8,128)(2,1)} %slice.225), channel_id=1, source_target_pairs={{0,2},{2,0},{4,6},{6,4},{8,10},{10,8},{12,14},{14,12},{16,18},{18,... | collective-permute-start | bytes 3932168 | tf_op jit(solution)/shard_map/ppermute | solution.py:92
  424.6 52.3 %collective-permute-start.39 = (bf16[1024,640]{1,0:T(8,128)(2,1)S(1)}, bf16[1024,640]{1,0:T(8,128)(2,1)S(1)}, u32[]{:S(2)}, u32[]{:S(2)}) collective-permute-start(bf16[1024,640]{1,0:T(8,128)(2,1)S(1)} %slice.217), channel_id=1, source_target_pairs={{0,2},{2,0},{4,6},{6,4},{8,10},{10,8},{12,14},{14,12},{16,18},{18,... | collective-permute-start | bytes 3932168 | tf_op jit(solution)/shard_map/ppermute | solution.py:92
  459.8 29.9 %collective-permute-start.34 = (bf16[128,640]{1,0:T(8,128)(2,1)S(1)}, bf16[128,640]{1,0:T(8,128)(2,1)S(1)}, u32[]{:S(2)}, u32[]{:S(2)}) collective-permute-start(bf16[128,640]{1,0:T(8,128)(2,1)S(1)} %slice.262), channel_id=1, source_target_pairs={{0,16},{2,18},{4,20},{6,22},{8,24},{10,26},{12,28},{14,30},{16,0},... | collective-permute-start | bytes 491528 | tf_op jit(solution)/shard_map/ppermute | solution.py:92
  501.9 49.8 %collective-permute-start.62 = (bf16[240,960]{1,0:T(8,128)(2,1)}, bf16[240,960]{1,0:T(8,128)(2,1)}, u32[]{:S(2)}, u32[]{:S(2)}) collective-permute-start(bf16[240,960]{1,0:T(8,128)(2,1)} %pad_maximum_fusion.17), channel_id=1, source_target_pairs={{0,2},{2,0},{4,6},{6,4},{8,10},{10,8},{12,14},{14,12},{16,18},{18,... | collective-permute-start | bytes 1382408 | tf_op jit(solution)/shard_map/ppermute | solution.py:92
  540.0 36.3 %collective-permute-start.47 = (bf16[2,240,704]{1,2,0:T(8,128)(2,1)}, bf16[2,240,704]{1,2,0:T(8,128)(2,1)}, u32[]{:S(2)}, u32[]{:S(2)}) collective-permute-start(bf16[2,240,704]{1,2,0:T(8,128)(2,1)} %fusion.68), channel_id=1, source_target_pairs={{0,2},{2,0},{4,6},{6,4},{8,10},{10,8},{12,14},{14,12},{16,18},{18,... | collective-permute-start | bytes 2027528 | tf_op jit(solution)/shard_map/ppermute | solution.py:92
  584.0 37.7 %collective-permute-start.80 = (bf16[240,640]{1,0:T(8,128)(2,1)S(1)}, bf16[240,640]{1,0:T(8,128)(2,1)S(1)}, u32[]{:S(2)}, u32[]{:S(2)}) collective-permute-start(bf16[240,640]{1,0:T(8,128)(2,1)S(1)} %add_convert_fusion.19), channel_id=1, source_target_pairs={{0,16},{2,18},{4,20},{6,22},{8,24},{10,26},{12,28},{14,30},{16,0},... | collective-permute-start | bytes 921608 | tf_op jit(solution)/shard_map/ppermute | solution.py:92
  593.1 45.1 %collective-permute-start.86 = (bf16[160,960]{0,1:T(8,128)(2,1)S(1)}, bf16[160,960]{0,1:T(8,128)(2,1)S(1)}, u32[]{:S(2)}, u32[]{:S(2)}) collective-permute-start(bf16[160,960]{0,1:T(8,128)(2,1)S(1)} %add_convert_fusion.13), channel_id=1, source_target_pairs={{0,16},{2,18},{4,20},{6,22},{8,24},{10,26},{12,28},{14,30},{16,0},... | collective-permute-start | bytes 921608 | tf_op jit(solution)/shard_map/ppermute | solution.py:92
  594.9 56.5 %collective-permute-start.75 = (bf16[240,640]{1,0:T(8,128)(2,1)S(1)}, bf16[240,640]{1,0:T(8,128)(2,1)S(1)}, u32[]{:S(2)}, u32[]{:S(2)}) collective-permute-start(bf16[240,640]{1,0:T(8,128)(2,1)S(1)} %add_convert_fusion.20), channel_id=1, source_target_pairs={{0,4},{2,6},{4,0},{6,2},{8,12},{10,14},{12,8},{14,10},{16,20},{18,... | collective-permute-start | bytes 921608 | tf_op jit(solution)/shard_map/ppermute | solution.py:92
  621.8 30.5 %collective-permute-start.81 = (bf16[240,640]{1,0:T(8,128)(2,1)S(1)}, bf16[240,640]{1,0:T(8,128)(2,1)S(1)}, u32[]{:S(2)}, u32[]{:S(2)}) collective-permute-start(bf16[240,640]{1,0:T(8,128)(2,1)S(1)} %add_convert_fusion.18), channel_id=1, source_target_pairs={{0,8},{2,10},{4,12},{6,14},{8,0},{10,2},{12,4},{14,6},{16,24},{18,... | collective-permute-start | bytes 921608 | tf_op jit(solution)/shard_map/ppermute | solution.py:92
  (152 other events, 1437.6 us)
